TPU v7x, 128 devices: a whole 4x4x4 slice. The times are simulated.
128 devices in a mesh: dp: 8 (over x, y_lo), tensor: 16 (over y_hi, z, core).
Axes of the slice: x: 4, y: 4 (y_hi: 2, y_lo: 2; y = y_hi * 2 + y_lo), z: 4, core: 2. Of those that a mesh axis runs over, the one named last changes fastest.
Arguments:
- tokens: bfloat16 [2560, 6144], P('dp', 'tensor'), may hold values from -6 to 6
- cotangent: bfloat16 [2560, 6144], P('dp', 'tensor'), may hold values from -6 to 6
- decor_matrix: float32 [6144, 6144], P('dp', 'tensor'), may hold values from -1 to 2
- in_weight: bfloat16 [6144, 12288], P(None, 'tensor'), may hold values from -0.078125 to 0.078125
- out_weight: bfloat16 [12288, 6144], P('tensor'), may hold values from -0.0546875 to 0.0546875
- lengths: int32 [8, 8], replicated, may hold values from 1 to 60, as said below
Outputs:
- layer_output: bfloat16 [2560, 6144], P('dp', 'tensor')
- input_grad: bfloat16 [2560, 6144], P('dp', 'tensor')
- decor_step: float32 [6144, 6144], P('dp', 'tensor')
Inputs may be any that keep to these rules, and one draw needn't show every extreme that they name: `lengths`: each row sums to at most 320; exactly one row sums to 320; all rows together sum to 128 times the number of data ranks.
All inputs are finite; a program needn't handle non-finite values.
Results may differ from a plain program's by a relative error of at most 0.03.
Values may be sent and summed in bfloat16 or wider, within the bound.
No kernel may reach another device: no remote copies, remote signals or barrier semaphores. Data moves between devices by JAX's collectives and lax.ppermute only.
A program may use at most 128 MiB of HBM per device.

v0:
```python
import math

import jax
import jax.numpy as jnp
from jax import lax
from jax.sharding import PartitionSpec as P

GELU_SCALE = math.sqrt(2.0 / math.pi)
GELU_CUBIC = 0.044715
EXACT_PRECISION = lax.Precision.HIGHEST
CONTRACT_LAST = (((1,), (1,)), ((), ()))
CONTRACT_FIRST = (((0,), (0,)), ((), ()))


def gelu_pair(values):
    inner_arg = GELU_SCALE * (values + GELU_CUBIC * values * values * values)
    tangent = jnp.tanh(inner_arg)
    output = 0.5 * values * (1.0 + tangent)
    gelu_slope = 0.5 * (1.0 + tangent) + 0.5 * values * (1.0 - tangent * tangent) * GELU_SCALE * (
        1.0 + 3.0 * GELU_CUBIC * values * values
    )
    return (output, gelu_slope)


def token_weights(lengths, rank_list, row_count):
    flat_lengths = lengths.reshape(-1)
    live_counts = jnp.sum(lengths, axis=1)
    rank_starts = jnp.cumsum(live_counts) - live_counts
    local_index = jnp.arange(row_count, dtype=jnp.int32)
    rank_match = rank_list[:, None] == jnp.arange(lengths.shape[0], dtype=jnp.int32)[None, :]
    rank_start = jnp.sum(jnp.where(rank_match, rank_starts[None, :], 0), axis=1)
    rank_limit = jnp.sum(jnp.where(rank_match, live_counts[None, :], 0), axis=1)
    packed_index = rank_start[:, None] + local_index[None, :]
    is_valid = local_index[None, :] < rank_limit[:, None]
    packed_index = packed_index.reshape(-1)
    seq_ends = jnp.cumsum(flat_lengths)
    seq_starts = seq_ends - flat_lengths
    member = (packed_index[:, None] >= seq_starts[None, :]) & (
        packed_index[:, None] < seq_ends[None, :]
    )
    seq_share = 1.0 / (lengths.shape[1] * flat_lengths.astype(jnp.float32))
    weight = jnp.sum(jnp.where(member, seq_share[None, :], 0.0), axis=1)
    is_valid = is_valid.reshape(-1)
    return (jnp.where(is_valid, weight, 0.0), is_valid)


def whiten_total(partial_value):
    return lax.psum(partial_value.astype(jnp.bfloat16), "tensor")


def local(tokens, cotangent, decor_matrix, in_weight, out_weight, lengths):
    own_rank = lax.axis_index("dp")
    row_total = tokens.shape[0]
    own_weights, own_valid = token_weights(lengths, own_rank.reshape(1), row_total)
    decor_columns = lax.all_gather(decor_matrix, "dp", axis=0, tiled=True)
    partial_value = lax.dot_general(
        tokens.astype(jnp.float32),
        decor_columns,
        CONTRACT_LAST,
        precision=EXACT_PRECISION,
        preferred_element_type=jnp.float32,
    )
    whitened = whiten_total(partial_value)
    dense_whitened = whitened.astype(jnp.float32)
    mixed_rows = jnp.dot(
        dense_whitened, decor_columns, precision=EXACT_PRECISION, preferred_element_type=jnp.float32
    )
    weighted_mixed = mixed_rows * own_weights[:, None]
    local_product = lax.dot_general(
        dense_whitened,
        weighted_mixed,
        CONTRACT_FIRST,
        precision=EXACT_PRECISION,
        preferred_element_type=jnp.float32,
    )
    local_diagonal = jnp.sum(own_weights[:, None] * dense_whitened * dense_whitened, axis=0)
    product, diagonal = (
        lax.psum_scatter(local_product, "dp", scatter_dimension=0, tiled=True),
        lax.psum_scatter(local_diagonal, "dp", scatter_dimension=0, tiled=True),
    )
    decor_step = product - diagonal[:, None] * decor_matrix
    pre_act = jnp.dot(whitened, in_weight, preferred_element_type=jnp.float32)
    gelu_out, gelu_slope = gelu_pair(pre_act)
    hidden = gelu_out.astype(jnp.bfloat16)
    out_partial = jnp.dot(hidden, out_weight, preferred_element_type=jnp.float32)
    back_hidden = lax.dot_general(
        lax.all_gather(cotangent, "tensor", axis=1, tiled=True),
        out_weight,
        CONTRACT_LAST,
        preferred_element_type=jnp.float32,
    )
    delta_hidden = (back_hidden * gelu_slope).astype(jnp.bfloat16)
    grad_partial = lax.dot_general(
        delta_hidden, in_weight, CONTRACT_LAST, preferred_element_type=jnp.float32
    )
    out_sum, grad_sum = (
        lax.psum_scatter(
            out_partial.astype(jnp.bfloat16), "tensor", scatter_dimension=1, tiled=True
        ).astype(jnp.float32),
        lax.psum_scatter(
            grad_partial.astype(jnp.bfloat16), "tensor", scatter_dimension=1, tiled=True
        ).astype(jnp.float32),
    )
    valid_column = own_valid[:, None]
    out_rows = jnp.where(valid_column, out_sum, 0.0).astype(jnp.bfloat16)
    grad_rows = jnp.where(valid_column, grad_sum, 0.0).astype(jnp.bfloat16)
    return (out_rows, grad_rows, decor_step)


def solution(mesh):
    placed = (
        P("dp", "tensor"),
        P("dp", "tensor"),
        P("dp", "tensor"),
        P(None, "tensor"),
        P("tensor", None),
        P(),
    )
    return jax.shard_map(
        local,
        mesh=mesh,
        in_specs=placed,
        out_specs=(P("dp", "tensor"), P("dp", "tensor"), P("dp", "tensor")),
        check_vma=False,
    )
```

profile of v0, /device:TPU:16, one launch (start us, length us, event | category | flops | bytes accessed | tf_op | source)
XLA Modules:
  0.0 812.0 jit_solution(16200398843076487639)
XLA Ops:
  7.2 0.0 copy-start
  7.2 0.0 all-gather.3.cloned.1.call-start
  7.2 0.7 all-gather.3.cloned.1.call-update
  7.9 0.0 all-reduce.3.cloned.1.call-start
  8.0 191.6 %all-gather.3.cloned.1.call-done = f32[6144,384]{1,0:T(8,128)} async-done(((f32[768,384]{1,0:T(8,128)}), f32[6144,384]{1,0:T(8,128)}) %all-gather.3.cloned.1.call-update) | async-done | bytes 9437200 | tf_op jit(solution)/shard_map/all_gather | solution.py:55
  199.6 0.0 copy-done
  199.6 10.1 %convolution_convert_fusion.2 = bf16[320,6144]{1,0:T(8,128)(2,1)} fusion(bf16[320,384]{1,0:T(8,128)(2,1)S(1)} %copy-done, f32[6144,384]{1,0:T(8,128)} %all-gather.3.cloned.1.call-done), kind=kOutput, calls=%fused_computation.3 | convolution fusion | flops 9061662720 | bytes 13615104 | tf_op jit(solution)/shard_map/dot_general | solution.py:56
  209.7 0.0 all-reduce.3.cloned.1.call-update
  209.7 0.0 all-gather.5.cloned.1.call-start
  209.8 0.7 all-gather.5.cloned.1.call-update
  210.5 0.0 reduce-scatter.12.cloned.1.call-start
  210.5 150.0 %all-reduce.3.cloned.1.call-done = bf16[320,6144]{1,0:T(8,128)(2,1)} async-done(((bf16[320,6144]{1,0:T(8,128)(2,1)}), bf16[320,6144]{1,0:T(8,128)(2,1)}) %all-reduce.3.cloned.1.call-update) | async-done | bytes 3932176 | tf_op jit(solution)/shard_map/psum | solution.py:48
  360.5 8.1 fusion.17
  368.5 49.4 %all-gather.5.cloned.1.call-done = bf16[320,6144]{1,0:T(8,128)(2,1)} async-done(((bf16[320,384]{1,0:T(8,128)(2,1)}), bf16[320,6144]{1,0:T(8,128)(2,1)}) %all-gather.5.cloned.1.call-update) | async-done | bytes 3932176 | tf_op jit(solution)/shard_map/all_gather | solution.py:87
  417.9 8.5 %fusion.1 = bf16[320,768]{1,0:T(8,128)(2,1)S(1)} fusion(bf16[320,6144]{1,0:T(8,128)(2,1)} %all-gather.5.cloned.1.call-done, bf16[768,6144]{1,0:T(8,128)(2,1)} %param.10, f32[320,768]{1,0:T(8,128)S(1)} %fusion.17), kind=kOutput, calls=%fused_computation.8 | convolution fusion | flops 3024568320 | bytes 14843904 | tf_op jit(solution)/shard_map/dot_general | solution.py:86
  426.4 11.4 %convolution_convert_fusion = bf16[320,6144]{1,0:T(8,128)(2,1)} fusion(bf16[320,768]{1,0:T(8,128)(2,1)S(1)} %fusion.1, bf16[6144,768]{1,0:T(8,128)(2,1)} %param.9), kind=kOutput, calls=%fused_computation.1 | convolution fusion | flops 3021864960 | bytes 13860864 | tf_op jit(solution)/shard_map/dot_general | solution.py:93
  437.8 6.4 copy.15
  444.2 0.0 reduce-scatter.12.cloned.1.call-update
  444.2 0.2 reduce-scatter.10.cloned.1.call-start
  444.5 8.6 %convolution_convert_fusion.1 = bf16[320,6144]{1,0:T(8,128)(2,1)} fusion(bf16[768,6144]{1,0:T(8,128)(2,1)} %param.10, f32[320,768]{1,0:T(8,128)S(1)} %fusion.17), kind=kOutput, calls=%fused_computation.2 | convolution fusion | flops 3024076800 | bytes 14352384 | tf_op jit(solution)/shard_map/dot_general | solution.py:85
  453.0 0.0 copy-start.4
  453.0 6.6 copy.13
  459.6 0.0 reduce-scatter.10.cloned.1.call-update
  459.7 0.0 reduce-scatter.8.cloned.1.call-start
  459.7 0.0 copy-done.4
  459.7 0.1 reshape.121
  459.8 0.1 reshape.120
  459.9 0.1 reduce_sum.45
  460.0 0.2 reduce-window.15
  460.2 0.1 reduce-window.16
  460.3 0.1 reduce.3
  460.4 0.6 fusion.12
  461.0 0.6 iota_add_fusion
  461.7 0.1 select_reduce_fusion
  461.8 0.7 broadcast_select_fusion
  462.5 0.0 copy-start.2
  462.5 10.2 %convolution_multiply_fusion.1 = f32[320,384]{1,0:T(8,128)S(1)} fusion(bf16[320,6144]{1,0:T(8,128)(2,1)} %all-reduce.3.cloned.1.call-done, f32[6144,384]{1,0:T(8,128)} %all-gather.3.cloned.1.call-done, f32[320]{0:T(512)S(1)} %broadcast_select_fusion), kind=kOutput, calls=%fused_computation.9 | convolution fusion | flops 9059819520 | bytes 13862144 | tf_op jit(solution)/shard_map/dot_general | solution.py:65
  472.8 0.0 copy-done.2
  472.8 11.3 %fusion.18 = f32[6144,384]{1,0:T(8,128)} fusion(bf16[320,6144]{1,0:T(8,128)(2,1)S(1)} %copy-done.2, f32[320,384]{1,0:T(8,128)S(1)} %convolution_multiply_fusion.1), kind=kOutput, calls=%fused_computation.38 | convolution fusion | flops 9059696640 | bytes 13860864 | tf_op jit(solution)/shard_map/dot_general | solution.py:69
  484.0 0.0 copy-start.5
  484.0 0.0 reduce-scatter.8.cloned.1.call-update
  484.1 0.0 copy-start.3
  484.1 0.6 copy-done.5
  484.7 0.6 dynamic-slice
  485.9 0.0 copy-start.1
  485.9 0.7 iota_compare_fusion
  486.6 3.4 fusion
  490.0 34.8 %all-reduce = f32[6144]{0:T(1024)S(1)} all-reduce(f32[6144]{0:T(1024)S(1)} %fusion), channel_id=5, replica_groups=mesh['dp'=8,'tensor'=16] {'dp'}, use_global_device_ids=true, to_apply=%region_11.12.clone | all-reduce | flops 6144 | bytes 49152
  524.8 0.1 dynamic-slice.1
  524.9 1.1 reduce-scatter.12.cloned.1.call-done
  525.9 1.1 copy.16
  527.1 84.4 %reduce-scatter.10.cloned.1.call-done = bf16[384,320]{1,0:T(8,128)(2,1)} async-done(((bf16[6144,320]{1,0:T(8,128)(2,1)}), bf16[384,320]{1,0:T(8,128)(2,1)}) %reduce-scatter.10.cloned.1.call-update) | async-done | bytes 245776
  611.5 1.1 copy.14
  612.7 0.9 select_convert_fusion
  613.6 189.1 %reduce-scatter.8.cloned.1.call-done = f32[768,384]{1,0:T(8,128)} async-done(((f32[6144,384]{1,0:T(8,128)}), f32[768,384]{1,0:T(8,128)}) %reduce-scatter.8.cloned.1.call-update) | async-done | bytes 1179664 | tf_op jit(solution)/shard_map/reduce_scatter | solution.py:78
  802.7 0.0 copy-done.3
  802.7 2.5 multiply_subtract_fusion
  805.2 0.0 copy-done.1
  (2 shorter events, 0.0 us)
Async XLA Ops:
  7.2 192.4 %copy-start = (bf16[320,384]{1,0:T(8,128)(2,1)S(1)}, bf16[320,384]{1,0:T(8,128)(2,1)}, u32[]{:S(2)}) copy-start(bf16[320,384]{1,0:T(8,128)(2,1)} %param.6) | copy-start | bytes 737284
  7.2 192.4 %all-gather.3.cloned.1.call-start = ((), (), s32[]{:S(2)}) async-start(), calls=%async_computation.3 | async-start | bytes 10616832 | tf_op jit(solution)/shard_map/all_gather | solution.py:55
  7.9 352.5 %all-reduce.3.cloned.1.call-start = ((), (), s32[]{:S(2)}) async-start(), calls=%async_computation.4 | async-start | bytes 7864320 | tf_op jit(solution)/shard_map/psum | solution.py:48
  209.7 208.2 %all-gather.5.cloned.1.call-start = ((), (), s32[]{:S(2)}) async-start(), calls=%async_computation.5 | async-start | bytes 4177920 | tf_op jit(solution)/shard_map/all_gather | solution.py:87
  210.5 315.5 %reduce-scatter.12.cloned.1.call-start = ((), (), s32[]{:S(2)}) async-start(), calls=%async_computation.8 | async-start | bytes 5013504
  444.2 167.3 %reduce-scatter.10.cloned.1.call-start = ((), (), s32[]{:S(2)}) async-start(), calls=%async_computation.7 | async-start | bytes 5013504
  453.0 6.7 copy-start.4
  459.7 343.1 %reduce-scatter.8.cloned.1.call-start = ((), (), s32[]{:S(2)}) async-start(), calls=%async_computation.6 | async-start | bytes 10616832 | tf_op jit(solution)/shard_map/reduce_scatter | solution.py:78
  462.5 10.3 %copy-start.2 = (bf16[320,6144]{1,0:T(8,128)(2,1)S(1)}, bf16[320,6144]{1,0:T(8,128)(2,1)}, u32[]{:S(2)}) copy-start(bf16[320,6144]{1,0:T(8,128)(2,1)} %all-reduce.3.cloned.1.call-done) | copy-start | bytes 11796484
  484.0 0.7 copy-start.5
  484.1 318.7 %copy-start.3 = (f32[768,384]{1,0:T(8,128)S(1)}, f32[768,384]{1,0:T(8,128)}, u32[]{:S(2)}) copy-start(f32[768,384]{1,0:T(8,128)} %param.8) | copy-start | bytes 3538948
  485.9 319.3 %copy-start.1 = (bf16[320,384]{1,0:T(8,128)(2,1)S(1)}, bf16[320,384]{1,0:T(8,128)(2,1)}, u32[]{:S(2)}) copy-start(bf16[320,384]{1,0:T(8,128)(2,1)} %param.6) | copy-start | bytes 737284
Sparse Core Ops, SparseCore 0:
  9.7 189.8 all-gather.2
  209.8 150.5 all-reduce.2
  363.0 54.8 all-gather.4
  444.4 81.5 reduce-scatter.11
  529.9 81.5 reduce-scatter.9
  613.9 188.7 reduce-scatter.7
where the time goes:
time: 814 us; the launch traced here: 812 us
  waiting for transfers between devices  667 us (82%)
  matrix products  68.2 us (8%)
  blocking collectives  34.8 us (4%)
  local copies, waits for them, and re-layouts  16.7 us (2%)
  between operations  14.9 us (2%)
  other arithmetic  10 us (1%)
    all_gather x1, waiting for transfers between devices, local(): decor_columns = lax.all_gather(decor_matrix, 'dp', axis=0, tiled=True)  192 us
    reduce_scatter x1, waiting for transfers between devices, local(): lax.psum_scatter(local_product, 'dp', scatter_dimension=0, tiled=True)  189 us
    psum x1, waiting for transfers between devices, whiten_total(): return lax.psum(partial_value.astype(jnp.bfloat16), 'tensor')  150 us
    unnamed x8, waiting for transfers between devices  87 us
    all_gather x1, waiting for transfers between devices, local(): lax.all_gather(cotangent, 'tensor', axis=1, tiled=True)  49.4 us
    unnamed x1, blocking collectives  34.8 us
    unnamed x18, local copies, waits for them, and re-layouts  16.6 us
  transfers between devices with their start and end apart: 6, of which 6 were waited for; matrix products, arithmetic and copies ran while one was open for 7% of the time, Pallas kernels for 0%

commit v1 on v0

v1 whole, which is shorter than its diff:
```python
import math

import jax
import jax.numpy as jnp
from jax import lax
from jax.sharding import Mesh, PartitionSpec as P

GELU_SCALE = math.sqrt(2.0 / math.pi)
GELU_CUBIC = 0.044715
BF16 = jnp.bfloat16
F32 = jnp.float32
CONTRACT_LAST = (((1,), (1,)), ((), ()))
CONTRACT_FIRST = (((0,), (0,)), ((), ()))
DP = ("x", "yl")
CHIPS = ("yh", "z")
CORE = "core"
N_DP = 8
N_CHIP = 8
GROUP = 128
PART = 8


def gelu_pair(values):
    inner_arg = GELU_SCALE * (values + GELU_CUBIC * values * values * values)
    tangent = jnp.tanh(inner_arg)
    output = 0.5 * values * (1.0 + tangent)
    gelu_slope = 0.5 * (1.0 + tangent) + 0.5 * values * (1.0 - tangent * tangent) * GELU_SCALE * (
        1.0 + 3.0 * GELU_CUBIC * values * values
    )
    return (output, gelu_slope)


def packed_weights(lengths, packed_index):
    flat_lengths = lengths.reshape(-1)
    seq_ends = jnp.cumsum(flat_lengths)
    seq_starts = seq_ends - flat_lengths
    member = (packed_index[:, None] >= seq_starts[None, :]) & (
        packed_index[:, None] < seq_ends[None, :]
    )
    seq_share = 1.0 / (lengths.shape[1] * flat_lengths.astype(F32))
    return jnp.sum(jnp.where(member, seq_share[None, :], 0.0), axis=1)


def split_bf16(values):
    high = lax.reduce_precision(values, 8, 7)
    return (high.astype(BF16), (values - high).astype(BF16))


def dot(left, right, numbers=(((1,), (0,)), ((), ()))):
    return lax.dot_general(left, right, numbers, preferred_element_type=F32)


def swap_core(value):
    return lax.ppermute(value, CORE, [(0, 1), (1, 0)])


def local(tokens, cotangent, decor_matrix, in_weight, out_weight, lengths):
    row_total, width = tokens.shape
    own_rank = lax.axis_index(DP)
    core = lax.axis_index(CORE)
    first_core = core == 0

    other_matrix = swap_core(decor_matrix)

    live = jnp.sum(lengths, axis=1)
    starts = jnp.cumsum(live) - live
    own_start = lax.dynamic_index_in_dim(starts, own_rank, keepdims=False)
    own_live = lax.dynamic_index_in_dim(live, own_rank, keepdims=False)

    local_row = jnp.arange(row_total, dtype=jnp.int32)
    own_packed = jnp.where(local_row < own_live, own_start + local_row, -1)
    all_packed = jnp.where(
        local_row[None, :] < live[:, None], starts[:, None] + local_row[None, :], -1
    ).reshape(-1)

    half_row = jnp.arange(N_CHIP * N_DP * PART, dtype=jnp.int32)
    half_base = (
        (half_row // PART) % N_DP * GROUP
        + half_row // (PART * N_DP) * (2 * PART)
        + half_row % PART
    )
    own_half = half_base + core * PART
    other_half = half_base + (1 - core) * PART

    pack = (jnp.arange(N_DP * GROUP, dtype=jnp.int32)[:, None] == own_packed[None, :]).astype(BF16)
    cot_placed = dot(pack, cotangent).astype(BF16).reshape(N_DP, GROUP, width)
    sent = jnp.concatenate(
        [jnp.broadcast_to(tokens[None], (N_DP,) + tokens.shape), cot_placed], axis=1
    )
    got = lax.all_to_all(sent, DP, 0, 0, tiled=True)
    all_tokens = got[:, :row_total].reshape(N_DP * row_total, width)
    cot_packed = jnp.sum(got[:, row_total:].astype(F32), axis=0).astype(BF16)

    pick_own = (own_half[:, None] == all_packed[None, :]).astype(BF16)
    pick_other = (other_half[:, None] == all_packed[None, :]).astype(BF16)
    far_tokens = swap_core(dot(pick_other, all_tokens).astype(BF16))
    near_tokens = dot(pick_own, all_tokens).astype(BF16)

    own_high, own_low = split_bf16(decor_matrix)
    far_high, far_low = split_bf16(other_matrix)
    partial_white = (
        dot(near_tokens, own_high, CONTRACT_LAST)
        + dot(near_tokens, own_low, CONTRACT_LAST)
        + dot(far_tokens, far_high, CONTRACT_LAST)
        + dot(far_tokens, far_low, CONTRACT_LAST)
    ).astype(BF16)

    chunk = N_DP * PART
    partial_white = partial_white.reshape(N_CHIP, chunk, 2 * width)
    sent = jnp.concatenate(
        [
            partial_white[:, :, :width],
            partial_white[:, :, width:],
            jnp.broadcast_to(cot_packed[None], (N_CHIP,) + cot_packed.shape),
        ],
        axis=1,
    )
    got = lax.all_to_all(sent, CHIPS, 0, 0, tiled=True)
    cot_near = got[:, 2 * chunk :]
    cot_far = swap_core(cot_near)
    white_sum = jnp.sum(got[:, : 2 * chunk].astype(F32), axis=0).astype(BF16)
    white_chunk = jnp.concatenate([white_sum[:chunk], white_sum[chunk:]], axis=1)

    white_part = lax.all_to_all(
        white_chunk.reshape(N_DP, PART, 2 * width), DP, 0, 0, tiled=True
    ).reshape(chunk, 2 * width)

    sent = jnp.broadcast_to(
        jnp.concatenate([white_part, white_chunk], axis=0)[None], (N_CHIP, 2 * chunk, 2 * width)
    )
    near = lax.all_to_all(sent, CHIPS, 0, 0, tiled=True)
    far = swap_core(near)

    white_rows = jnp.concatenate([near[:, chunk:], far[:, chunk:]], axis=0).reshape(
        N_DP * GROUP, 2 * width
    )
    row_weights = packed_weights(lengths, jnp.concatenate([own_half, other_half]))
    mixed_part = (dot(white_rows, own_high) + dot(white_rows, own_low)).astype(BF16)
    mixed_got = lax.all_to_all(mixed_part.reshape(N_DP, GROUP, width), DP, 0, 0, tiled=True)
    mixed_own = jnp.sum(mixed_got.astype(F32), axis=0).astype(BF16)
    white_float = white_rows.astype(F32)
    diagonal = jnp.sum(row_weights[:, None] * white_float * white_float, axis=0)

    def rows_of(block):
        block = block.reshape(N_CHIP, N_DP, PART, 2 * width)
        return jnp.transpose(block, (0, 2, 1, 3)).reshape(N_CHIP, PART, N_DP * 2 * width)

    ff_near, ff_far = rows_of(near[:, :chunk]), rows_of(far[:, :chunk])
    whitened = jnp.stack(
        [jnp.where(first_core, ff_near, ff_far), jnp.where(first_core, ff_far, ff_near)], axis=1
    ).reshape(GROUP, N_DP * 2 * width)
    cot_pair = jnp.stack(
        [jnp.where(first_core, cot_near, cot_far), jnp.where(first_core, cot_far, cot_near)], axis=1
    )
    cot_full = jnp.transpose(cot_pair, (2, 0, 1, 3)).reshape(GROUP, N_CHIP * 2 * width)

    pre_act = dot(whitened, in_weight)
    gelu_out, gelu_slope = gelu_pair(pre_act)
    hidden = gelu_out.astype(BF16)
    back_hidden = dot(cot_full, out_weight, CONTRACT_LAST)
    delta_hidden = (back_hidden * gelu_slope).astype(BF16)
    out_partial = dot(hidden, out_weight).astype(BF16)
    grad_partial = dot(delta_hidden, in_weight, CONTRACT_LAST).astype(BF16)

    both = jnp.stack([out_partial, grad_partial]).reshape(2, GROUP, N_CHIP, 2, width)
    kept = lax.dynamic_index_in_dim(both, core, 3, keepdims=False)
    given = lax.dynamic_index_in_dim(both, 1 - core, 3, keepdims=False)
    summed = (kept.astype(F32) + swap_core(given).astype(F32)).astype(BF16)
    sent = jnp.transpose(summed, (2, 0, 1, 3)).reshape(N_CHIP, 2 * GROUP, width)
    got = lax.all_to_all(sent, CHIPS, 0, 0, tiled=True)
    out_own = jnp.sum(got.astype(F32), axis=0).astype(BF16)

    sent = jnp.concatenate([out_own, mixed_own], axis=0)
    sent = jnp.broadcast_to(sent[None], (N_DP,) + sent.shape)
    got = lax.all_to_all(sent, DP, 0, 0, tiled=True)
    mixed = got[:, 2 * GROUP :].reshape(N_DP * GROUP, width)
    weighted_mixed = (mixed.astype(F32) * row_weights[:, None]).astype(BF16)
    product = dot(white_rows, weighted_mixed, CONTRACT_FIRST)
    decor_step = product - diagonal[:, None] * decor_matrix

    unpack = (own_packed[:, None] == jnp.arange(N_DP * GROUP, dtype=jnp.int32)[None, :]).astype(BF16)
    out_rows = dot(unpack, got[:, :GROUP].reshape(N_DP * GROUP, width)).astype(BF16)
    grad_rows = dot(unpack, got[:, GROUP : 2 * GROUP].reshape(N_DP * GROUP, width)).astype(BF16)
    return (out_rows, grad_rows, decor_step)


def solution(mesh):
    fine = Mesh(mesh.devices.reshape(4, 2, 2, 4, 2), ("x", "yl", "yh", "z", "core"))
    tensor = ("yh", "z", "core")
    placed = (
        P(DP, tensor),
        P(DP, tensor),
        P(DP, tensor),
        P(None, tensor),
        P(tensor, None),
        P(),
    )
    return jax.shard_map(
        local,
        mesh=fine,
        in_specs=placed,
        out_specs=(P(DP, tensor), P(DP, tensor), P(DP, tensor)),
        check_vma=False,
    )
```

time: 814 us -> 274 us (0.34)
  waiting for transfers between devices: 667 us -> 107 us
  blocking collectives: 34.8 us -> 61.8 us
  matrix products: 68.2 us -> 41.8 us
  starting transfers between devices: 0.42 us -> 21 us
  between operations: 14.9 us -> 1.12 us
  other arithmetic: 10 us -> 18.7 us
    all_gather x2 -> x0, waiting for transfers between devices: 241 us -> none  [the longest x1 192 us: local(): decor_columns = lax.all_gather(decor_matrix, 'dp', axis=0, tiled=True)]
    reduce_scatter x1 -> x0, waiting for transfers between devices: 189 us -> none  [local(): lax.psum_scatter(local_product, 'dp', scatter_dimension=0, tiled=True)]
    psum x1 -> x0, waiting for transfers between devices: 150 us -> none  [whiten_total(): return lax.psum(partial_value.astype(jnp.bfloat16), 'tensor')]
    all_to_all x0 -> x4, waiting for transfers between devices: none -> 103 us  [the longest x2 74 us: local(): got = lax.all_to_all(sent, DP, 0, 0, tiled=True)]
    unnamed x8 -> x0, waiting for transfers between devices: 87 us -> none
    all_to_all x0 -> x3, blocking collectives: none -> 61.8 us  [the longest x1 28.6 us: local(): got = lax.all_to_all(sent, CHIPS, 0, 0, tiled=True)]
    unnamed x1 -> x0, blocking collectives: 34.8 us -> none
    dot_general x7 -> x15, matrix products: 68.2 us -> 41.8 us  [dot(): return lax.dot_general(left, right, numbers, preferred_element_type=F32)]
  transfers between devices with their start and end apart: 6 -> 9, of which waited for: 6 -> 6; matrix products, arithmetic and copies ran while one was open for 7% -> 7% of each run, Pallas kernels for 0% -> 0%
where the time goes in v1:
time: 274 us; the launch traced here: 273 us
  waiting for transfers between devices  107 us (39%)
  blocking collectives  61.8 us (23%)
  matrix products  41.8 us (15%)
  local copies, waits for them, and re-layouts  22.3 us (8%)
  starting transfers between devices  21 us (8%)
  other arithmetic  18.7 us (7%)
    all_to_all x2, waiting for transfers between devices, local(): got = lax.all_to_all(sent, DP, 0, 0, tiled=True)  74 us
    dot_general x15, matrix products, dot(): return lax.dot_general(left, right, numbers, preferred_element_type=F32)  41.8 us
    all_to_all x1, blocking collectives, local(): got = lax.all_to_all(sent, CHIPS, 0, 0, tiled=True)  28.6 us
    all_to_all x1, blocking collectives, local(): near = lax.all_to_all(sent, CHIPS, 0, 0, tiled=True)  24.5 us
    all_to_all x1, waiting for transfers between devices, local(): got = lax.all_to_all(sent, CHIPS, 0, 0, tiled=True)  18.7 us
    all_to_all x1, waiting for transfers between devices, local(): lax.all_to_all(mixed_part.reshape(N_DP, GROUP, width), DP, 0, 0, tiled=True)  10.3 us
    all_to_all x2, starting transfers between devices, local(): got = lax.all_to_all(sent, DP, 0, 0, tiled=True)  9.52 us
    all_to_all x1, blocking collectives, local(): lax.all_to_all(white_chunk.reshape(N_DP, PART, 2 * width), DP, 0, 0, tile...  8.69 us
  transfers between devices with their start and end apart: 9, of which 6 were waited for; matrix products, arithmetic and copies ran while one was open for 7% of the time, Pallas kernels for 0%

profile of v1, /device:TPU:16, one launch (start us, length us, event | category | flops | bytes accessed | tf_op | source)
XLA Modules:
  0.0 273.5 jit_solution(5753079664065378898)
XLA Ops:
  0.7 0.9 reduce_sum.75
  1.5 0.6 dynamic_slice.14
  2.1 0.2 reduce-window.14
  2.3 0.6 dynamic_slice.15
  2.9 1.3 add_select_fusion.4
  4.2 0.6 fusion.11
  4.8 0.2 broadcast_in_dim.26
  5.0 1.8 pad_maximum_fusion
  6.8 5.0 %all-to-all-start = ((bf16[8,448,384]{2,1,0:T(8,128)(2,1)}), bf16[8,448,384]{2,1,0:T(8,128)(2,1)S(1)}, u32[]{:S(2)}, u32[]{:S(2)}) async-start(bf16[8,448,384]{2,1,0:T(8,128)(2,1)} %pad_maximum_fusion), calls=%async_computation | async-start | bytes 5505024 | tf_op jit(solution)/shard_map/all_to_all | solution.py:90
  12.0 40.0 %all-to-all-done = bf16[8,448,384]{2,1,0:T(8,128)(2,1)S(1)} async-done(((bf16[8,448,384]{2,1,0:T(8,128)(2,1)}), bf16[8,448,384]{2,1,0:T(8,128)(2,1)S(1)}, u32[]{:S(2)}, u32[]{:S(2)}) %all-to-all-start) | async-done | bytes 2752544 | tf_op jit(solution)/shard_map/all_to_all | solution.py:90
  52.0 0.2 slice.60
  52.2 2.3 fusion.17
  54.6 1.6 fusion.14
  56.2 1.8 fusion.59
  58.2 2.0 fusion.47
  60.2 2.0 fusion.32
  62.2 1.9 add_convert_fusion.1
  64.2 0.4 copy.45
  64.6 0.4 copy.46
  65.1 0.7 pad_maximum_fusion.1
  65.8 28.6 %all_to_all.35 = bf16[8,256,384]{1,2,0:T(8,128)(2,1)S(1)} all-to-all(bf16[8,256,384]{1,2,0:T(8,128)(2,1)S(1)} %pad_maximum_fusion.1), channel_id=1, replica_groups=mesh['x'=4,'yl'=2,'yh'=2,'z'=4,'core'=2] {'yh','z'}, dimensions={0} | all-to-all | bytes 3145728 | tf_op jit(solution)/shard_map/all_to_all | solution.py:118
  94.7 2.3 collective-permute-done.3
  96.9 1.6 select_bitcast_fusion.1
  98.8 8.7 %all_to_all.36 = bf16[8,8,768]{2,1,0:T(8,128)(2,1)S(1)} all-to-all(bf16[8,8,768]{2,1,0:T(8,128)(2,1)S(1)} %bitcast.81), channel_id=1, replica_groups=mesh['x'=4,'yl'=2,'yh'=2,'z'=4,'core'=2] {'x','yl'}, dimensions={0} | all-to-all | bytes 196608 | tf_op jit(solution)/shard_map/all_to_all | solution.py:124
  107.5 0.2 copy.38
  107.8 0.1 copy.39
  108.1 24.5 %all_to_all.37 = bf16[8,128,768]{2,1,0:T(8,128)(2,1)S(1)} all-to-all(bf16[8,128,768]{2,1,0:T(8,128)(2,1)S(1)} %broadcast_in_dim.28), channel_id=1, replica_groups=mesh['x'=4,'yl'=2,'yh'=2,'z'=4,'core'=2] {'yh','z'}, dimensions={0} | all-to-all | bytes 3145728 | tf_op jit(solution)/shard_map/all_to_all | solution.py:131
  132.6 2.1 pad_maximum_fusion.3
  134.7 1.4 collective-permute-done.2
  136.1 2.1 broadcast_select_fusion.1
  138.2 0.1 pad_maximum_fusion.2
  138.4 5.3 %fusion.86 = f32[128,768]{1,0:T(8,128)S(1)} fusion(bf16[128,6144]{1,0:T(8,128)(2,1)S(1)} %bitcast.66, bf16[6144,768]{1,0:T(8,128)(2,1)} %param.9), kind=kOutput, calls=%fused_computation.130 | convolution fusion | flops 1207959552 | bytes 11403264 | tf_op jit(solution)/shard_map/dot_general | solution.py:50
  143.7 0.7 slice-done.1
  144.4 0.2 slice-done.2
  144.6 2.6 convolution_convert_fusion.1
  147.2 14.4 %convolution_convert_fusion = bf16[128,6144]{1,0:T(8,128)(2,1)} fusion(bf16[6144,768]{1,0:T(8,128)(2,1)} %param.9, bf16[128,6144]{0,1:T(8,128)(2,1)S(1)} %bitcast.65, bf16[768,6144]{1,0:T(8,128)(2,1)} %param.10, f32[128,768]{1,0:T(8,128)} %copy-done.11), kind=kOutput, calls=%fused_computation | convolution fusion | flops 2418573312 | bytes 22413312 | tf_op jit(solution)/shard_map/dot_general | solution.py:50
  161.6 5.0 %stack.28 = bf16[1,128,8,2,384]{4,3,2,1,0:T(2,128)(2,1)} reshape(bf16[128,6144]{1,0:T(8,128)(2,1)} %convolution_convert_fusion) | data formatting | bytes 3145728 | tf_op jit(solution)/shard_map/stack | solution.py:165
  166.7 2.0 stack.24
  168.7 1.7 copy_dynamic-update-slice_fusion.1
  170.4 0.1 copy-done.7
  170.6 0.4 copy_dynamic-update-slice_fusion
  171.0 1.5 dynamic-slice_bitcast_fusion
  172.4 0.7 copy-done.4
  173.2 0.1 pad_maximum_fusion.4
  173.4 1.6 copy-done.3
  175.0 1.0 fusion.57
  176.0 1.9 add_convert_fusion
  177.9 4.2 %all-to-all-start.5 = ((bf16[8,128,384]{2,1,0:T(8,128)(2,1)}), bf16[8,128,384]{2,1,0:T(8,128)(2,1)}, u32[]{:S(2)}, u32[]{:S(2)}) async-start(bf16[8,128,384]{2,1,0:T(8,128)(2,1)} %bitcast.71), calls=%async_computation.5 | async-start | bytes 1572864 | tf_op jit(solution)/shard_map/all_to_all | solution.py:139
  182.1 2.3 fusion.5
  184.4 1.4 copy.43
  185.8 10.3 %all-to-all-done.5 = bf16[8,128,384]{2,1,0:T(8,128)(2,1)} async-done(((bf16[8,128,384]{2,1,0:T(8,128)(2,1)}), bf16[8,128,384]{2,1,0:T(8,128)(2,1)}, u32[]{:S(2)}, u32[]{:S(2)}) %all-to-all-start.5) | async-done | bytes 786464 | tf_op jit(solution)/shard_map/all_to_all | solution.py:139
  196.1 7.1 %all-to-all-start.4 = ((bf16[8,256,384]{2,1,0:T(8,128)(2,1)}), bf16[8,256,384]{2,1,0:T(8,128)(2,1)}, u32[]{:S(2)}, u32[]{:S(2)}) async-start(bf16[8,256,384]{2,1,0:T(8,128)(2,1)} %copy.43), calls=%async_computation.4 | async-start | bytes 3145728 | tf_op jit(solution)/shard_map/all_to_all | solution.py:170
  203.1 1.2 reduce_sum.79
  204.4 18.7 %all-to-all-done.4 = bf16[8,256,384]{2,1,0:T(8,128)(2,1)} async-done(((bf16[8,256,384]{2,1,0:T(8,128)(2,1)}), bf16[8,256,384]{2,1,0:T(8,128)(2,1)}, u32[]{:S(2)}, u32[]{:S(2)}) %all-to-all-start.4) | async-done | bytes 1572896 | tf_op jit(solution)/shard_map/all_to_all | solution.py:170
  223.1 1.7 reduce_sum.78
  224.8 1.6 broadcast_in_dim.29
  226.4 4.5 %all-to-all-start.6 = ((bf16[8,384,384]{2,1,0:T(8,128)(2,1)}), bf16[8,384,384]{2,1,0:T(8,128)(2,1)}, u32[]{:S(2)}, u32[]{:S(2)}) async-start(bf16[8,384,384]{2,1,0:T(8,128)(2,1)} %broadcast_in_dim.29), calls=%async_computation.6 | async-start | bytes 4718592 | tf_op jit(solution)/shard_map/all_to_all | solution.py:175
  231.5 0.5 fusion.4
  232.1 33.9 %all-to-all-done.6 = bf16[8,384,384]{2,1,0:T(8,128)(2,1)} async-done(((bf16[8,384,384]{2,1,0:T(8,128)(2,1)}), bf16[8,384,384]{2,1,0:T(8,128)(2,1)}, u32[]{:S(2)}, u32[]{:S(2)}) %all-to-all-start.6) | async-done | bytes 2359328 | tf_op jit(solution)/shard_map/all_to_all | solution.py:175
  266.0 1.6 fusion.83
  267.6 1.2 fusion.21
  268.8 1.2 fusion.20
  270.1 1.3 multiply_convert_fusion
  271.4 2.0 convolution_subtract_fusion
  (64 shorter events, 2.1 us)
Async XLA Ops:
  0.6 3.6 %copy-start = (bf16[320,384]{1,0:T(8,128)(2,1)S(1)}, bf16[320,384]{1,0:T(8,128)(2,1)}, u32[]{:S(2)}) copy-start(bf16[320,384]{1,0:T(8,128)(2,1)} %param.7) | copy-start | bytes 737284
  0.6 4.2 %copy-start.13 = (bf16[320,384]{1,0:T(8,128)(2,1)S(1)}, bf16[320,384]{1,0:T(8,128)(2,1)}, u32[]{:S(2)}) copy-start(bf16[320,384]{1,0:T(8,128)(2,1)} %param.6) | copy-start | bytes 737284
  6.8 45.2 %all-to-all-start = ((bf16[8,448,384]{2,1,0:T(8,128)(2,1)}), bf16[8,448,384]{2,1,0:T(8,128)(2,1)S(1)}, u32[]{:S(2)}, u32[]{:S(2)}) async-start(bf16[8,448,384]{2,1,0:T(8,128)(2,1)} %pad_maximum_fusion), calls=%async_computation | async-start | bytes 5505024 | tf_op jit(solution)/shard_map/all_to_all | solution.py:90
  11.9 48.3 %collective-permute-start.1 = (f32[768,384]{1,0:T(8,128)}, f32[768,384]{1,0:T(8,128)}, u32[]{:S(2)}, u32[]{:S(2)}) collective-permute-start(f32[768,384]{1,0:T(8,128)} %param.8), channel_id=1, source_target_pairs={{0,1},{1,0},{2,3},{3,2},{4,5},{5,4},{6,7},{7,6},{8,9},{9,8},{10,11... | collective-permute-start | bytes 3538952 | tf_op jit(solution)/shard_map/ppermute | solution.py:54
  54.6 5.6 %collective-permute-start = (bf16[512,384]{1,0:T(8,128)(2,1)}, bf16[512,384]{1,0:T(8,128)(2,1)S(1)}, u32[]{:S(2)}, u32[]{:S(2)}) collective-permute-start(bf16[512,384]{1,0:T(8,128)(2,1)} %fusion.17), channel_id=1, source_target_pairs={{0,1},{1,0},{2,3},{3,2},{4,5},{5,4},{6,7},{7,6},{8,9},{9,8},{10,11... | collective-permute-start | bytes 1179656 | tf_op jit(solution)/shard_map/ppermute | solution.py:54
  54.6 1.6 copy-start.2
  56.1 1.8 copy-start.12
  60.2 2.0 copy-start.5
  94.6 2.4 collective-permute-start.3
  132.6 2.1 copy-start.10
  132.6 3.5 %collective-permute-start.2 = (bf16[8,128,768]{2,1,0:T(8,128)(2,1)S(1)}, bf16[8,128,768]{2,1,0:T(8,128)(2,1)}, u32[]{:S(2)}, u32[]{:S(2)}) collective-permute-start(bf16[8,128,768]{2,1,0:T(8,128)(2,1)S(1)} %all_to_all.37), channel_id=1, source_target_pairs={{0,1},{1,0},{2,3},{3,2},{4,5},{5,4},{6,7},{7,6},{8,9},{9,8},{10,11... | collective-permute-start | bytes 4718600 | tf_op jit(solution)/shard_map/ppermute | solution.py:54
  138.2 5.5 %slice-start = ((s8[9437184]{0:T(1024)(128)(4,1)}), s8[4194304]{0:T(1024)(128)(4,1)S(1)}, s32[]{:S(2)}) async-start(s8[9437184]{0:T(1024)(128)(4,1)} %bitcast.63), calls=%async_computation.7 | async-start | bytes 8388608
  138.3 6.0 %slice-start.1 = ((s8[9437184]{0:T(1024)(128)(4,1)}), s8[4194304]{0:T(1024)(128)(4,1)S(1)}, s32[]{:S(2)}) async-start(s8[9437184]{0:T(1024)(128)(4,1)} %bitcast.63), calls=%async_computation.8 | async-start | bytes 8388608
  138.4 6.2 %slice-start.2 = ((s8[9437184]{0:T(1024)(128)(4,1)}), s8[1048576]{0:T(1024)(128)(4,1)S(1)}, s32[]{:S(2)}) async-start(s8[9437184]{0:T(1024)(128)(4,1)} %bitcast.63), calls=%async_computation.9 | async-start | bytes 2097152
  144.6 2.6 copy-start.11
  161.6 5.0 %copy-start.6 = (bf16[128,6144]{1,0:T(8,128)(2,1)S(1)}, bf16[128,6144]{1,0:T(8,128)(2,1)}, u32[]{:S(2)}) copy-start(bf16[128,6144]{1,0:T(8,128)(2,1)} %convolution_convert_fusion.1) | copy-start | bytes 4718596
  168.7 1.9 copy-start.7
  170.9 2.2 copy-start.4
  173.1 9.0 %collective-permute-start.4 = (bf16[2,128,8,384]{3,2,1,0:T(8,128)(2,1)}, bf16[2,128,8,384]{3,2,1,0:T(8,128)(2,1)}, u32[]{:S(2)}, u32[]{:S(2)}) collective-permute-start(bf16[2,128,8,384]{3,2,1,0:T(8,128)(2,1)} %dynamic-slice_bitcast_fusion), channel_id=1, source_target_pairs={{0,1},{1,0},{2,3},{3,2},{4,5},{5,4},{6,7},{7,6},{8,9},{9,8},{10,11... | collective-permute-start | bytes 4718600 | tf_op jit(solution)/shard_map/ppermute | solution.py:54
  173.2 1.8 copy-start.3
  173.4 2.6 copy-start.8
  177.9 18.2 %all-to-all-start.5 = ((bf16[8,128,384]{2,1,0:T(8,128)(2,1)}), bf16[8,128,384]{2,1,0:T(8,128)(2,1)}, u32[]{:S(2)}, u32[]{:S(2)}) async-start(bf16[8,128,384]{2,1,0:T(8,128)(2,1)} %bitcast.71), calls=%async_computation.5 | async-start | bytes 1572864 | tf_op jit(solution)/shard_map/all_to_all | solution.py:139
  196.1 27.1 %all-to-all-start.4 = ((bf16[8,256,384]{2,1,0:T(8,128)(2,1)}), bf16[8,256,384]{2,1,0:T(8,128)(2,1)}, u32[]{:S(2)}, u32[]{:S(2)}) async-start(bf16[8,256,384]{2,1,0:T(8,128)(2,1)} %copy.43), calls=%async_computation.4 | async-start | bytes 3145728 | tf_op jit(solution)/shard_map/all_to_all | solution.py:170
  226.4 4.5 %copy-start.14 = (s32[8,8]{1,0:T(8,128)S(1)}, s32[8,8]{1,0:T(8,128)}, u32[]{:S(2)}) copy-start(s32[8,8]{1,0:T(8,128)} %param.11) | copy-start | bytes 772
  226.4 39.6 %all-to-all-start.6 = ((bf16[8,384,384]{2,1,0:T(8,128)(2,1)}), bf16[8,384,384]{2,1,0:T(8,128)(2,1)}, u32[]{:S(2)}, u32[]{:S(2)}) async-start(bf16[8,384,384]{2,1,0:T(8,128)(2,1)} %broadcast_in_dim.29), calls=%async_computation.6 | async-start | bytes 4718592 | tf_op jit(solution)/shard_map/all_to_all | solution.py:175
  268.8 2.6 copy-start.9
  271.4 2.0 copy-start.1

commit v2 on v1

v2 whole, which is shorter than its diff:
```python
import math

import jax
import jax.numpy as jnp
from jax import lax
from jax.experimental import pallas as pl
from jax.experimental.pallas import tpu as pltpu
from jax.sharding import Mesh, PartitionSpec as P

GELU_SCALE = math.sqrt(2.0 / math.pi)
GELU_CUBIC = 0.044715
BF16 = jnp.bfloat16
F32 = jnp.float32
CONTRACT_LAST = (((1,), (1,)), ((), ()))
CONTRACT_FIRST = (((0,), (0,)), ((), ()))
DP = ("x", "yl")
CHIPS = ("yh", "z")
CORE = "core"
N_DP = 8
N_CHIP = 8
GROUP = 128
PART = 8
HALF = 64
ROWS = 1024
CHUNK = 768
SLOTS = 48
WEIGHT_COPIES = 4


def gelu_pair(values):
    inner_arg = GELU_SCALE * (values + GELU_CUBIC * values * values * values)
    tangent = jnp.tanh(inner_arg)
    output = 0.5 * values * (1.0 + tangent)
    gelu_slope = 0.5 * (1.0 + tangent) + 0.5 * values * (1.0 - tangent * tangent) * GELU_SCALE * (
        1.0 + 3.0 * GELU_CUBIC * values * values
    )
    return (output, gelu_slope)


def packed_weights(lengths, packed_index):
    flat_lengths = lengths.reshape(-1)
    seq_ends = jnp.cumsum(flat_lengths)
    seq_starts = seq_ends - flat_lengths
    member = (packed_index[:, None] >= seq_starts[None, :]) & (
        packed_index[:, None] < seq_ends[None, :]
    )
    seq_share = 1.0 / (lengths.shape[1] * flat_lengths.astype(F32))
    return jnp.sum(jnp.where(member, seq_share[None, :], 0.0), axis=1)


def split_bf16(values):
    high = lax.reduce_precision(values, 8, 7)
    return (high.astype(BF16), (values - high).astype(BF16))


def dot(left, right, numbers=(((1,), (0,)), ((), ()))):
    return lax.dot_general(left, right, numbers, preferred_element_type=F32)


def swap_core(value):
    return lax.ppermute(value, CORE, [(0, 1), (1, 0)])


def mixed_kernel(core_ref, near_ref, far_ref, high_ref, low_ref, rows_ref, mixed_ref):
    own = pl.multiple_of(core_ref[0] * HALF, HALF)
    other = pl.multiple_of(HALF - core_ref[0] * HALF, HALF)
    for group in range(N_DP):
        columns = pl.ds(group * CHUNK, CHUNK)
        rows_ref[group, pl.ds(own, HALF), :] = near_ref[:, columns]
        rows_ref[group, pl.ds(other, HALF), :] = far_ref[:, columns]
    rows = rows_ref[...].reshape(ROWS, CHUNK)
    total = dot(rows, high_ref[...]) + dot(rows, low_ref[...])
    mixed_ref[...] = total.astype(BF16).reshape(mixed_ref.shape)


def mixed_terms(core, near, far, high, low):
    vmem = pl.BlockSpec(memory_space=pltpu.VMEM)
    return pl.pallas_call(
        mixed_kernel,
        in_specs=[pl.BlockSpec(memory_space=pltpu.SMEM)] + [vmem] * 4,
        out_specs=[vmem, vmem],
        out_shape=[
            jax.ShapeDtypeStruct((N_DP, GROUP, CHUNK), BF16),
            jax.ShapeDtypeStruct((N_DP, GROUP, high.shape[1]), BF16),
        ],
        compiler_params=pltpu.CompilerParams(vmem_limit_bytes=16 << 20),
        cost_estimate=pl.CostEstimate(
            flops=4 * ROWS * CHUNK * 384, bytes_accessed=5 << 20, transcendentals=0
        ),
        name="mixed_terms",
    )(core, near, far, high, low)


def feed_kernel(
    core_ref, near_ref, far_ref, cot_near_ref, cot_far_ref, in_ref, out_ref, kept_ref, given_ref,
    in_buf, out_buf, rows_buf, cot_buf, hidden_buf, delta_buf, in_sem, out_sem,
):
    own = pl.multiple_of(core_ref[0] * HALF, HALF)
    other = pl.multiple_of(HALF - core_ref[0] * HALF, HALF)
    first_core = core_ref[0] == 0
    steps = kept_ref.shape[0]
    width = CHUNK // 2
    in_copies, out_copies = [], []
    for step in range(WEIGHT_COPIES):
        rows = pl.ds(step * (in_buf.shape[0] // WEIGHT_COPIES), in_buf.shape[0] // WEIGHT_COPIES)
        in_copies.append(
            pltpu.make_async_copy(in_ref.at[rows, :], in_buf.at[rows, :], in_sem.at[step])
        )
        columns = pl.ds(
            step * (out_buf.shape[1] // WEIGHT_COPIES), out_buf.shape[1] // WEIGHT_COPIES
        )
        out_copies.append(
            pltpu.make_async_copy(out_ref.at[:, columns], out_buf.at[:, columns], out_sem.at[step])
        )
    for step in range(WEIGHT_COPIES):
        out_copies[step].start()
        in_copies[step].start()
    rows_buf[pl.ds(own, HALF), :] = near_ref[...]
    rows_buf[pl.ds(other, HALF), :] = far_ref[...]
    for step in range(steps):
        for half in range(2):
            lanes = pl.ds(half * width, width)
            close, away = cot_near_ref[step, :, lanes], cot_far_ref[step, :, lanes]
            rows = pl.ds(half * HALF, HALF)
            cot_buf[rows, pl.ds(step * CHUNK, width)] = jnp.where(first_core, close, away)
            cot_buf[rows, pl.ds(step * CHUNK + width, width)] = jnp.where(first_core, away, close)
    pre_act, back = 0.0, 0.0
    depth = in_buf.shape[0] // WEIGHT_COPIES
    for step in range(WEIGHT_COPIES):
        span = pl.ds(step * depth, depth)
        out_copies[step].wait()
        back = back + dot(cot_buf[:, span], out_buf[:, span], CONTRACT_LAST)
        in_copies[step].wait()
        pre_act = pre_act + dot(rows_buf[:, span], in_buf[span, :])
    gelu_out, gelu_slope = gelu_pair(pre_act)
    hidden_buf[...] = gelu_out.astype(BF16)
    delta_buf[...] = (back * gelu_slope).astype(BF16)

    def store(step, place, value):
        left, right = value[:, :width], value[:, width:]
        rows = pl.ds(place, GROUP)
        kept_ref[step, rows, :] = jnp.where(first_core, left, right).astype(BF16)
        given_ref[step, rows, :] = jnp.where(first_core, right, left).astype(BF16)

    for step in range(steps):
        columns = pl.ds(step * CHUNK, CHUNK)
        store(step, GROUP, dot(delta_buf[...], in_buf[columns, :], CONTRACT_LAST))
    for step in range(steps):
        columns = pl.ds(step * CHUNK, CHUNK)
        store(step, 0, dot(hidden_buf[...], out_buf[:, columns]))


def feed_forward(core, near, far, cot_near, cot_far, in_weight, out_weight):
    vmem = pl.BlockSpec(memory_space=pltpu.VMEM)
    anywhere = pl.BlockSpec(memory_space=pl.ANY)
    steps = in_weight.shape[0] // CHUNK
    hidden = in_weight.shape[1]
    part = jax.ShapeDtypeStruct((steps, 2 * GROUP, CHUNK // 2), BF16)
    return pl.pallas_call(
        feed_kernel,
        in_specs=[pl.BlockSpec(memory_space=pltpu.SMEM)] + [vmem] * 4 + [anywhere] * 2,
        out_specs=[vmem, vmem],
        out_shape=[part, part],
        scratch_shapes=[
            pltpu.VMEM(in_weight.shape, BF16),
            pltpu.VMEM(out_weight.shape, BF16),
            pltpu.VMEM((GROUP, steps * CHUNK), BF16),
            pltpu.VMEM((GROUP, steps * CHUNK), BF16),
            pltpu.VMEM((GROUP, hidden), BF16),
            pltpu.VMEM((GROUP, hidden), BF16),
            pltpu.SemaphoreType.DMA((WEIGHT_COPIES,)),
            pltpu.SemaphoreType.DMA((WEIGHT_COPIES,)),
        ],
        compiler_params=pltpu.CompilerParams(vmem_limit_bytes=46 << 20),
        cost_estimate=pl.CostEstimate(flops=1 << 20, bytes_accessed=1 << 16, transcendentals=0),
        name="feed_forward",
    )(core, near, far, cot_near, cot_far, in_weight, out_weight)


def rank_spans(lengths_ref):
    live, starts, total = [], [], 0
    for rank in range(N_DP):
        count = lengths_ref[rank, 0]
        for column in range(1, lengths_ref.shape[1]):
            count = count + lengths_ref[rank, column]
        live.append(count)
        starts.append(total)
        total = total + count
    return live, starts


def entry_of(values, rank):
    found = values[0]
    for place in range(1, N_DP):
        found = jnp.where(rank == place, values[place], found)
    return found


def first_row(group, start):
    return lax.rem(group + ROWS - start, N_DP)


def one_hot(condition):
    return condition.astype(F32).astype(BF16)


def pack_kernel(place_ref, lengths_ref, tokens_ref, cot_ref, sent_ref):
    live, starts = rank_spans(lengths_ref)
    start, own_live = entry_of(starts, place_ref[0]), entry_of(live, place_ref[0])
    row_total, width = tokens_ref.shape
    slot = lax.broadcasted_iota(jnp.int32, (SLOTS, row_total), 0)
    row = lax.broadcasted_iota(jnp.int32, (SLOTS, row_total), 1)
    for group in range(N_DP):
        wanted = slot * N_DP + first_row(group, start)
        pick = one_hot((row == wanted) & (row < own_live))
        sent_ref[group, :, pl.ds(0, width)] = dot(pick, tokens_ref[...]).astype(BF16)
        sent_ref[group, :, pl.ds(width, width)] = dot(pick, cot_ref[...]).astype(BF16)


def group_kernel(place_ref, lengths_ref, got_ref, near_ref, given_ref, cot_ref, rows_buf):
    live, starts = rank_spans(lengths_ref)
    group, core = place_ref[0], place_ref[1]
    row = lax.broadcasted_iota(jnp.int32, (GROUP, SLOTS), 0)
    slot = lax.broadcasted_iota(jnp.int32, (GROUP, SLOTS), 1)
    total = jnp.zeros((GROUP, CHUNK), F32)
    for rank in range(N_DP):
        first = first_row(group, starts[rank])
        shift = (starts[rank] + first - group) // N_DP
        pick = one_hot((row == slot + shift) & (slot * N_DP + first < live[rank]))
        total = total + dot(pick, got_ref[rank])
    rows_buf[...] = total.astype(BF16)
    width = CHUNK // 2
    left, right = pl.ds(0, width), pl.ds(width, width)
    near_ref[...] = rows_buf[pl.ds(pl.multiple_of(core * HALF, HALF), HALF), left]
    given_ref[...] = rows_buf[pl.ds(pl.multiple_of(HALF - core * HALF, HALF), HALF), left]
    cot_ref[:, left] = rows_buf[pl.ds(0, HALF), right]
    cot_ref[:, right] = rows_buf[pl.ds(HALF, HALF), right]


def spread_kernel(place_ref, lengths_ref, got_ref, mixed_ref, sent_ref, rows_buf):
    live, starts = rank_spans(lengths_ref)
    group = place_ref[0]
    total = got_ref[0].astype(F32)
    for chip in range(1, N_CHIP):
        total = total + got_ref[chip].astype(F32)
    rows_buf[...] = total.astype(BF16)
    slot = lax.broadcasted_iota(jnp.int32, (SLOTS, GROUP), 0)
    row = lax.broadcasted_iota(jnp.int32, (SLOTS, GROUP), 1)
    for rank in range(N_DP):
        first = first_row(group, starts[rank])
        shift = (starts[rank] + first - group) // N_DP
        pick = one_hot((row == slot + shift) & (slot * N_DP + first < live[rank]))
        for half in range(2):
            rows = rows_buf[pl.ds(half * GROUP, GROUP), :]
            sent_ref[rank, pl.ds(half * SLOTS, SLOTS), :] = dot(pick, rows).astype(BF16)
        sent_ref[rank, pl.ds(2 * SLOTS, GROUP), :] = mixed_ref[...]


def final_kernel(
    place_ref, lengths_ref, got_ref, rows_ref, diagonal_ref, matrix_ref, out_ref, grad_ref, step_ref
):
    live, starts = rank_spans(lengths_ref)
    start, own_live = entry_of(starts, place_ref[0]), entry_of(live, place_ref[0])
    row_total, width = out_ref.shape
    row = lax.broadcasted_iota(jnp.int32, (row_total, SLOTS), 0)
    slot = lax.broadcasted_iota(jnp.int32, (row_total, SLOTS), 1)
    out_total = jnp.zeros((row_total, width), F32)
    grad_total = jnp.zeros((row_total, width), F32)
    for group in range(N_DP):
        wanted = slot * N_DP + first_row(group, start)
        pick = one_hot((row == wanted) & (row < own_live))
        out_total = out_total + dot(pick, got_ref[group, pl.ds(0, SLOTS), :])
        grad_total = grad_total + dot(pick, got_ref[group, pl.ds(SLOTS, SLOTS), :])
    out_ref[...] = out_total.astype(BF16)
    grad_ref[...] = grad_total.astype(BF16)
    mixed = got_ref[:, pl.ds(2 * SLOTS, GROUP), :].reshape(ROWS, width)
    product = dot(rows_ref[...], mixed, CONTRACT_FIRST)
    step_ref[...] = product - diagonal_ref[...] * matrix_ref[...]


def small_call(kernel, shapes, scratch, limit, *operands):
    smem = pl.BlockSpec(memory_space=pltpu.SMEM)
    vmem = pl.BlockSpec(memory_space=pltpu.VMEM)
    return pl.pallas_call(
        kernel,
        in_specs=[smem, smem] + [vmem] * (len(operands) - 2),
        out_specs=[vmem] * len(shapes),
        out_shape=shapes,
        scratch_shapes=scratch,
        compiler_params=pltpu.CompilerParams(vmem_limit_bytes=limit << 20),
        cost_estimate=pl.CostEstimate(flops=1 << 20, bytes_accessed=1 << 16, transcendentals=0),
        name=kernel.__name__,
    )(*operands)


def local(tokens, cotangent, decor_matrix, in_weight, out_weight, lengths):
    width = tokens.shape[1]
    own_rank = lax.axis_index(DP)
    core = lax.axis_index(CORE)
    core_list = core.reshape(1)
    place = jnp.stack([own_rank, core])

    def bf16_shape(*shape):
        return jax.ShapeDtypeStruct(shape, BF16)

    (sent,) = small_call(
        pack_kernel, [bf16_shape(N_DP, SLOTS, CHUNK)], [], 8, place, lengths, tokens, cotangent
    )
    got = lax.all_to_all(sent, DP, 0, 0, tiled=True)
    near_tokens, given_tokens, cot_packed = small_call(
        group_kernel,
        [bf16_shape(HALF, width), bf16_shape(HALF, width), bf16_shape(HALF, CHUNK)],
        [pltpu.VMEM((GROUP, CHUNK), BF16)],
        8,
        place,
        lengths,
        got,
    )

    pair_tokens = jnp.concatenate([near_tokens, swap_core(given_tokens)], axis=1)
    sent = jnp.broadcast_to(pair_tokens[None], (N_DP,) + pair_tokens.shape)
    got = lax.all_to_all(sent, DP, 0, 0, tiled=True)
    all_tokens = jnp.transpose(got.reshape(N_DP, N_CHIP, PART, CHUNK), (1, 0, 2, 3))

    own_high, own_low = split_bf16(decor_matrix)
    far_high = swap_core(own_high)
    pair_matrix = jnp.concatenate([own_high, far_high], axis=1)
    partial_white = dot(all_tokens.reshape(ROWS // 2, CHUNK), pair_matrix, CONTRACT_LAST)

    got = lax.all_to_all(
        partial_white.astype(BF16).reshape(N_CHIP, HALF, CHUNK), CHIPS, 0, 0, tiled=True
    )
    white_chunk = jnp.sum(got.astype(F32), axis=0).astype(BF16).reshape(N_DP, PART, CHUNK)

    white_part = lax.all_to_all(white_chunk, DP, 0, 0, tiled=True)

    sent = jnp.concatenate(
        [white_part.reshape(HALF, CHUNK), white_chunk.reshape(HALF, CHUNK), cot_packed], axis=0
    )
    sent = jnp.broadcast_to(sent[None], (N_CHIP,) + sent.shape)
    got = lax.all_to_all(sent, CHIPS, 0, 0, tiled=True)

    def wide_rows(block):
        block = block.reshape(N_CHIP, N_DP, PART, CHUNK)
        return jnp.transpose(block, (0, 2, 1, 3)).reshape(HALF, N_DP * CHUNK)

    decor_near = wide_rows(got[:, HALF : 2 * HALF])
    cot_near = got[:, 2 * HALF :]
    feed_near = wide_rows(got[:, :HALF])
    decor_far = swap_core(decor_near)
    cot_far = swap_core(cot_near)
    feed_far = swap_core(feed_near)

    group_row = jnp.arange(GROUP, dtype=jnp.int32) * N_DP
    all_rows = (jnp.arange(N_DP, dtype=jnp.int32)[:, None] + group_row[None, :]).reshape(-1)
    row_weights = packed_weights(lengths, all_rows)
    own_weights = packed_weights(lengths, own_rank + group_row)
    white_rows, mixed_part = mixed_terms(core_list, decor_near, decor_far, own_high, own_low)
    white_rows = white_rows.reshape(ROWS, CHUNK)
    mixed_got = lax.all_to_all(mixed_part, DP, 0, 0, tiled=True)
    mixed_own = jnp.sum(mixed_got.astype(F32), axis=0)
    weighted_own = (mixed_own * own_weights[:, None]).astype(BF16)
    white_float = white_rows.astype(F32)
    diagonal = jnp.sum(row_weights[:, None] * white_float * white_float, axis=0)
    feed_near = lax.optimization_barrier((feed_near, mixed_part))[0]

    kept, given = feed_forward(
        core_list, feed_near, feed_far, cot_near, cot_far, in_weight, out_weight
    )
    given = lax.optimization_barrier((given, mixed_got))[0]
    summed = (kept.astype(F32) + swap_core(given).astype(F32)).astype(BF16)
    got = lax.all_to_all(summed, CHIPS, 0, 0, tiled=True)

    (sent,) = small_call(
        spread_kernel,
        [bf16_shape(N_DP, 2 * SLOTS + GROUP, width)],
        [pltpu.VMEM((2 * GROUP, width), BF16)],
        12,
        place,
        lengths,
        got,
        weighted_own,
    )
    got = lax.all_to_all(sent, DP, 0, 0, tiled=True)
    return tuple(
        small_call(
            final_kernel,
            [
                bf16_shape(*tokens.shape),
                bf16_shape(*tokens.shape),
                jax.ShapeDtypeStruct(decor_matrix.shape, F32),
            ],
            [],
            16,
            place,
            lengths,
            got,
            white_rows,
            diagonal[:, None],
            decor_matrix,
        )
    )


def solution(mesh):
    fine = Mesh(mesh.devices.reshape(4, 2, 2, 4, 2), ("x", "yl", "yh", "z", "core"))
    tensor = ("yh", "z", "core")
    placed = (
        P(DP, tensor),
        P(DP, tensor),
        P(DP, tensor),
        P(None, tensor),
        P(tensor, None),
        P(),
    )
    return jax.shard_map(
        local,
        mesh=fine,
        in_specs=placed,
        out_specs=(P(DP, tensor), P(DP, tensor), P(DP, tensor)),
        check_vma=False,
    )
```

time: 274 us -> 197 us (0.72)
  waiting for transfers between devices: 107 us -> 57.2 us
  matrix products: 41.8 us -> 0.81 us
  Pallas kernels: 0 us -> 25 us
  blocking collectives: 61.8 us -> 75 us
  local copies, waits for them, and re-layouts: 22.3 us -> 9.73 us
  other arithmetic: 18.7 us -> 6.48 us
    all_to_all x2, waiting for transfers between devices: 74 us -> 32 us  [local(): got = lax.all_to_all(sent, DP, 0, 0, tiled=True)]
    dot_general x15 -> x1, matrix products: 41.8 us -> 0.81 us  [dot(): return lax.dot_general(left, right, numbers, preferred_element_type=F32)]
    pallas_call x0 -> x6, Pallas kernels: none -> 25 us  [the longest x1 15.6 us: feed_forward(): pl.pallas_call(feed_kernel, in_specs=[pl.BlockSpec(memory_space=pltpu.SME...]
    all_to_all x2 -> x3, blocking collectives: 33.2 us -> 43.7 us  [the longest x1 19 us: local(): lax.all_to_all(partial_white.astype(BF16).reshape(N_CHIP, HALF, CHUNK), C...]
    all_to_all x2, waiting for transfers between devices: 29 us -> 18.6 us  [the longest x1 18.6 us: local(): got = lax.all_to_all(summed, CHIPS, 0, 0, tiled=True)]
    another operation x4 -> x1, local copies, waits for them, and re-layouts: 7.51 us -> 0.07 us  [the longest x3 7.44 us: local(): jnp.stack([out_partial, grad_partial]).reshape(2, GROUP, N_CHIP, 2, width)]
    another operation x6 -> x3, other arithmetic: 4.22 us -> 0.28 us  [the longest x2 3.68 us: local(): jnp.stack([jnp.where(first_core, cot_near, cot_far), jnp.where(first_core...]
    select_n x3 -> x0, other arithmetic: 3.42 us -> none  [the longest x1 2.05 us: local(): jnp.where(first_core, ff_near, ff_far)]
  transfers between devices with their start and end apart: 9 -> 10, of which waited for: 6 -> 6; matrix products, arithmetic and copies ran while one was open for 7% -> 2% of each run, Pallas kernels for 0% -> 9%
where the time goes in v2:
time: 197 us
  blocking collectives  75 us (38%)
  waiting for transfers between devices  57.2 us (29%)
  Pallas kernels  25 us (13%)
  starting transfers between devices  21.4 us (11%)
  local copies, waits for them, and re-layouts  9.73 us (5%)
  other arithmetic  6.48 us (3%)
    all_to_all x2, waiting for transfers between devices, local(): got = lax.all_to_all(sent, DP, 0, 0, tiled=True)  32 us
    all_to_all x1, blocking collectives, local(): got = lax.all_to_all(sent, CHIPS, 0, 0, tiled=True)  31.4 us
    all_to_all x1, blocking collectives, local(): lax.all_to_all(partial_white.astype(BF16).reshape(N_CHIP, HALF, CHUNK), C...  19 us
    all_to_all x1, waiting for transfers between devices, local(): got = lax.all_to_all(summed, CHIPS, 0, 0, tiled=True)  18.6 us
    pallas_call x1, Pallas kernels, feed_forward(): pl.pallas_call(feed_kernel, in_specs=[pl.BlockSpec(memory_space=pltpu.SME...  15.6 us
    all_to_all x1, blocking collectives, local(): got = lax.all_to_all(sent, DP, 0, 0, tiled=True)  15.6 us
    all_to_all x2, starting transfers between devices, local(): got = lax.all_to_all(sent, DP, 0, 0, tiled=True)  9.56 us
    all_to_all x1, blocking collectives, local(): white_part = lax.all_to_all(white_chunk, DP, 0, 0, tiled=True)  9.04 us
  transfers between devices with their start and end apart: 10, of which 6 were waited for; matrix products, arithmetic and copies ran while one was open for 2% of the time, Pallas kernels for 9%

profile of v2, /device:TPU:16, one launch (start us, length us, event | category | flops | bytes accessed | tf_op | source)
XLA Modules:
  0.0 196.6 jit_solution(10324943886586117143)
XLA Ops:
  0.6 0.0 copy-start.11
  0.6 0.1 pad_add_fusion.place_ref
  0.7 0.9 copy-done.8
  1.7 0.9 copy-done.9
  2.6 0.7 copy-done.10
  3.3 1.4 pack_kernel.1
  4.7 15.6 %all_to_all.40.got_ref = bf16[8,48,768]{2,1,0:T(8,128)(2,1)S(1)} all-to-all(bf16[8,48,768]{2,1,0:T(8,128)(2,1)S(1)} %pack_kernel.1), channel_id=1, replica_groups=mesh['x'=4,'yl'=2,'yh'=2,'z'=4,'core'=2] {'x','yl'}, dimensions={0} | all-to-all | bytes 1179648 | tf_op jit(solution)/shard_map/all_to_all | solution.py:309
  20.4 0.0 copy-done.11
  20.4 1.2 group_kernel.1
  21.6 0.1 collective-permute-start
  21.7 1.2 collective-permute-done
  22.9 0.9 broadcast_in_dim.26
  23.9 3.5 %all-to-all-start.1 = ((bf16[8,64,768]{2,1,0:T(8,128)(2,1)}), bf16[8,64,768]{2,1,0:T(8,128)(2,1)S(1)}, u32[]{:S(2)}, u32[]{:S(2)}) async-start(bf16[8,64,768]{2,1,0:T(8,128)(2,1)} %broadcast_in_dim.26), calls=%async_computation.1 | async-start | bytes 1572864 | tf_op jit(solution)/shard_map/all_to_all | solution.py:322
  27.4 0.0 copy-done.1
  27.4 1.0 fusion.1
  28.4 0.2 collective-permute-start.1
  28.6 12.1 %all-to-all-done.1 = bf16[8,64,768]{2,1,0:T(8,128)(2,1)S(1)} async-done(((bf16[8,64,768]{2,1,0:T(8,128)(2,1)}), bf16[8,64,768]{2,1,0:T(8,128)(2,1)S(1)}, u32[]{:S(2)}, u32[]{:S(2)}) %all-to-all-start.1) | async-done | bytes 786464 | tf_op jit(solution)/shard_map/all_to_all | solution.py:322
  40.7 0.1 copy.15
  40.8 0.0 collective-permute-done.1
  40.8 0.8 convolution_convert_fusion
  41.6 0.0 copy-done.6
  41.6 19.0 %all_to_all.41 = bf16[8,64,768]{2,1,0:T(8,128)(2,1)S(1)} all-to-all(bf16[8,64,768]{2,1,0:T(8,128)(2,1)S(1)} %bitcast.32), channel_id=1, replica_groups=mesh['x'=4,'yl'=2,'yh'=2,'z'=4,'core'=2] {'yh','z'}, dimensions={0} | all-to-all | bytes 1572864 | tf_op jit(solution)/shard_map/all_to_all | solution.py:330
  60.6 0.1 reduce_sum.48
  60.7 9.0 %all_to_all.42 = bf16[8,8,768]{2,1,0:T(8,128)(2,1)S(1)} all-to-all(bf16[8,8,768]{2,1,0:T(8,128)(2,1)S(1)} %bitcast.30), channel_id=1, replica_groups=mesh['x'=4,'yl'=2,'yh'=2,'z'=4,'core'=2] {'x','yl'}, dimensions={0} | all-to-all | bytes 196608 | tf_op jit(solution)/shard_map/all_to_all | solution.py:335
  69.8 0.2 broadcast_in_dim.27
  70.0 31.4 %all_to_all.43 = bf16[8,192,768]{2,1,0:T(8,128)(2,1)S(1)} all-to-all(bf16[8,192,768]{2,1,0:T(8,128)(2,1)S(1)} %broadcast_in_dim.27), channel_id=1, replica_groups=mesh['x'=4,'yl'=2,'yh'=2,'z'=4,'core'=2] {'yh','z'}, dimensions={0} | all-to-all | bytes 4718592 | tf_op jit(solution)/shard_map/all_to_all | solution.py:341
  101.3 0.2 fusion.6
  101.5 0.1 collective-permute-start.2
  101.6 0.5 collective-permute-start.3
  102.1 0.1 collective-permute-start.4
  102.2 1.9 collective-permute-done.2.far_ref
  104.1 1.9 mixed_terms.1
  105.9 0.0 copy-start.4
  105.9 0.9 copy-done.4
  106.8 4.4 %all-to-all-start.5 = ((bf16[8,128,384]{2,1,0:T(8,128)(2,1)}), bf16[8,128,384]{2,1,0:T(8,128)(2,1)}, u32[]{:S(2)}, u32[]{:S(2)}) async-start(bf16[8,128,384]{2,1,0:T(8,128)(2,1)} %copy-done.4), calls=%async_computation.5 | async-start | bytes 1572864 | tf_op jit(solution)/shard_map/all_to_all | solution.py:360
  111.2 0.0 collective-permute-done.3.far_ref
  111.2 0.0 collective-permute-done.4.cot_far_ref
  111.2 15.6 %feed_forward.1 = (bf16[8,256,384]{2,1,0:T(8,128)(2,1)S(1)}, bf16[8,256,384]{2,1,0:T(8,128)(2,1)S(1)}) custom-call(s32[1]{0:T(128)} %bitcast.1.core_ref, bf16[64,6144]{1,0:T(8,128)(2,1)S(1)} %bitcast.26, bf16[64,6144]{1,0:T(8,128)(2,1)} %collective-permute-done.3.far_ref, bf16[8,64,768]{2,1,0:T(8,128)(2,1)S(1)} %get-tuple-element.21.cot_near_ref, ...), custom_call_target="tpu_custom_call" | custom-call | flops 1048576 | bytes 65536 | tf_op jit(solution)/shard_map/feed_forward/pallas_call | solution.py:159
  126.9 0.0 copy-start.3
  126.9 1.1 copy-done.3
  128.0 1.1 copy-done.12
  129.2 0.0 all-to-all-done.5
  129.2 0.1 collective-permute-start.5
  129.3 3.5 %collective-permute-done.5 = bf16[8,256,384]{2,1,0:T(8,128)(2,1)S(1)} collective-permute-done((bf16[8,256,384]{2,1,0:T(8,128)(2,1)}, bf16[8,256,384]{2,1,0:T(8,128)(2,1)S(1)}, u32[]{:S(2)}, u32[]{:S(2)}) %collective-permute-start.5) | collective-permute-done | bytes 1572896 | tf_op jit(solution)/shard_map/ppermute | solution.py:61
  132.8 2.9 %add_convert_fusion = bf16[8,256,384]{2,1,0:T(8,128)(2,1)} fusion(bf16[8,256,384]{2,1,0:T(8,128)(2,1)S(1)} %collective-permute-done.5, bf16[8,256,384]{2,1,0:T(8,128)(2,1)} %copy-done.3), kind=kLoop, calls=%fused_computation.2 | loop fusion | flops 3145728 | bytes 4718592 | tf_op jit(solution)/shard_map/convert_element_type | solution.py:371
  135.8 6.4 %all-to-all-start.6 = ((bf16[8,256,384]{2,1,0:T(8,128)(2,1)}), bf16[8,256,384]{2,1,0:T(8,128)(2,1)S(1)}, u32[]{:S(2)}, u32[]{:S(2)}) async-start(bf16[8,256,384]{2,1,0:T(8,128)(2,1)} %add_convert_fusion), calls=%async_computation.6 | async-start | bytes 3145728 | tf_op jit(solution)/shard_map/all_to_all | solution.py:372
  142.2 0.1 reshape.121
  142.2 0.1 reshape.119
  142.3 0.1 reduce-window.7
  142.4 0.1 reduce.2
  142.6 0.1 select_reduce_fusion.1
  142.7 1.3 convert_reduce_fusion
  143.9 0.1 multiply_convert_fusion.mixed_ref
  144.0 18.6 %all-to-all-done.6.got_ref = bf16[8,256,384]{2,1,0:T(8,128)(2,1)S(1)} async-done(((bf16[8,256,384]{2,1,0:T(8,128)(2,1)}), bf16[8,256,384]{2,1,0:T(8,128)(2,1)S(1)}, u32[]{:S(2)}, u32[]{:S(2)}) %all-to-all-start.6) | async-done | bytes 1572896 | tf_op jit(solution)/shard_map/all_to_all | solution.py:372
  162.6 1.2 spread_kernel.1
  163.8 0.0 copy-start
  163.8 1.1 copy-done
  164.9 6.0 %all-to-all-start.7 = ((bf16[8,224,384]{2,1,0:T(8,128)(2,1)}), bf16[8,224,384]{2,1,0:T(8,128)(2,1)S(1)}, u32[]{:S(2)}, u32[]{:S(2)}) async-start(bf16[8,224,384]{2,1,0:T(8,128)(2,1)} %copy-done), calls=%async_computation.7 | async-start | bytes 2752512 | tf_op jit(solution)/shard_map/all_to_all | solution.py:384
  171.0 0.1 select_reduce_fusion
  171.1 0.5 fusion
  171.6 0.2 broadcast_in_dim.58.diagonal_ref
  171.8 19.9 %all-to-all-done.7.got_ref = bf16[8,224,384]{2,1,0:T(8,128)(2,1)S(1)} async-done(((bf16[8,224,384]{2,1,0:T(8,128)(2,1)}), bf16[8,224,384]{2,1,0:T(8,128)(2,1)S(1)}, u32[]{:S(2)}, u32[]{:S(2)}) %all-to-all-start.7) | async-done | bytes 1376288 | tf_op jit(solution)/shard_map/all_to_all | solution.py:384
  191.7 1.3 copy-done.2
  193.0 3.6 %final_kernel.1 = (bf16[320,384]{1,0:T(8,128)(2,1)}, bf16[320,384]{1,0:T(8,128)(2,1)}, f32[768,384]{1,0:T(8,128)}) custom-call(s32[2]{0:T(128)S(1)} %pad_add_fusion.place_ref, s32[8,8]{1,0:T(8,128)S(1)} %copy-done.11, bf16[8,224,384]{2,1,0:T(8,128)(2,1)S(1)} %all-to-all-done.7.got_ref, bf16[1024,768]{1,0:T(8,128)(2,1)S(1)} %bitcast.24, ...), custom_call_target="tpu_custom_call" | custom-call | flops 1048576 | bytes 65536 | tf_op jit(solution)/shard_map/final_kernel/pallas_call | solution.py:284
  (18 shorter events, 0.1 us)
Async XLA Ops:
  0.6 19.8 %copy-start.11 = (s32[8,8]{1,0:T(8,128)S(1)}, s32[8,8]{1,0:T(8,128)}, u32[]{:S(2)}) copy-start(s32[8,8]{1,0:T(8,128)} %lengths_ref.7) | copy-start | bytes 772
  0.7 0.9 copy-start.8
  1.7 0.9 copy-start.9
  2.6 0.7 copy-start.10
  20.4 7.0 %copy-start.1 = (f32[768,384]{1,0:T(8,128)S(1)}, f32[768,384]{1,0:T(8,128)}, u32[]{:S(2)}) copy-start(f32[768,384]{1,0:T(8,128)} %matrix_ref.1) | copy-start | bytes 3538948
  21.6 1.3 collective-permute-start
  23.9 16.9 %all-to-all-start.1 = ((bf16[8,64,768]{2,1,0:T(8,128)(2,1)}), bf16[8,64,768]{2,1,0:T(8,128)(2,1)S(1)}, u32[]{:S(2)}, u32[]{:S(2)}) async-start(bf16[8,64,768]{2,1,0:T(8,128)(2,1)} %broadcast_in_dim.26), calls=%async_computation.1 | async-start | bytes 1572864 | tf_op jit(solution)/shard_map/all_to_all | solution.py:322
  28.4 13.2 %copy-start.6 = (bf16[768,384]{1,0:T(8,128)(2,1)}, bf16[768,384]{1,0:T(8,128)(2,1)S(1)}, u32[]{:S(2)}) copy-start(bf16[768,384]{1,0:T(8,128)(2,1)S(1)} %get-tuple-element.25.high_ref) | copy-start | bytes 1769476
  28.4 12.3 %collective-permute-start.1 = (bf16[768,384]{1,0:T(8,128)(2,1)S(1)}, bf16[768,384]{1,0:T(8,128)(2,1)S(1)}, u32[]{:S(2)}, u32[]{:S(2)}) collective-permute-start(bf16[768,384]{1,0:T(8,128)(2,1)S(1)} %get-tuple-element.25.high_ref), channel_id=1, source_target_pairs={{0,1},{1,0},{2,3},{3,2},{4,5},{5,4},{6,7},{7,6},{8,9},{9,8},{10,11... | collective-permute-start | bytes 1769480 | tf_op jit(solution)/shard_map/ppermute | solution.py:61
  101.3 2.7 %copy-start.5 = (bf16[768,384]{1,0:T(8,128)(2,1)S(1)}, bf16[768,384]{1,0:T(8,128)(2,1)}, u32[]{:S(2)}) copy-start(bf16[768,384]{1,0:T(8,128)(2,1)} %get-tuple-element.24.low_ref) | copy-start | bytes 1769476
  101.3 2.7 %copy-start.7 = (bf16[768,384]{1,0:T(8,128)(2,1)S(1)}, bf16[768,384]{1,0:T(8,128)(2,1)}, u32[]{:S(2)}) copy-start(bf16[768,384]{1,0:T(8,128)(2,1)} %copy-done.6) | copy-start | bytes 1769476
  101.5 2.6 %collective-permute-start.2 = (bf16[64,6144]{1,0:T(8,128)(2,1)S(1)}, bf16[64,6144]{1,0:T(8,128)(2,1)S(1)}, u32[]{:S(2)}, u32[]{:S(2)}) collective-permute-start(bf16[64,6144]{1,0:T(8,128)(2,1)S(1)} %bitcast.27), channel_id=1, source_target_pairs={{0,1},{1,0},{2,3},{3,2},{4,5},{5,4},{6,7},{7,6},{8,9},{9,8},{10,11... | collective-permute-start | bytes 2359304 | tf_op jit(solution)/shard_map/ppermute | solution.py:61
  101.6 9.6 %collective-permute-start.3 = (bf16[64,6144]{1,0:T(8,128)(2,1)S(1)}, bf16[64,6144]{1,0:T(8,128)(2,1)}, u32[]{:S(2)}, u32[]{:S(2)}) collective-permute-start(bf16[64,6144]{1,0:T(8,128)(2,1)S(1)} %bitcast.25), channel_id=1, source_target_pairs={{0,1},{1,0},{2,3},{3,2},{4,5},{5,4},{6,7},{7,6},{8,9},{9,8},{10,11... | collective-permute-start | bytes 2359304 | tf_op jit(solution)/shard_map/ppermute | solution.py:61
  102.1 9.1 %collective-permute-start.4 = (bf16[8,64,768]{2,1,0:T(8,128)(2,1)S(1)}, bf16[8,64,768]{2,1,0:T(8,128)(2,1)}, u32[]{:S(2)}, u32[]{:S(2)}) collective-permute-start(bf16[8,64,768]{2,1,0:T(8,128)(2,1)S(1)} %get-tuple-element.21.cot_near_ref), channel_id=1, source_target_pairs={{0,1},{1,0},{2,3},{3,2},{4,5},{5,4},{6,7},{7,6},{8,9},{9,8},{10,11... | collective-permute-start | bytes 2359304 | tf_op jit(solution)/shard_map/ppermute | solution.py:61
  105.9 0.9 copy-start.4
  106.8 22.4 %all-to-all-start.5 = ((bf16[8,128,384]{2,1,0:T(8,128)(2,1)}), bf16[8,128,384]{2,1,0:T(8,128)(2,1)}, u32[]{:S(2)}, u32[]{:S(2)}) async-start(bf16[8,128,384]{2,1,0:T(8,128)(2,1)} %copy-done.4), calls=%async_computation.5 | async-start | bytes 1572864 | tf_op jit(solution)/shard_map/all_to_all | solution.py:360
  126.9 1.2 copy-start.3
  128.0 1.2 copy-start.12
  129.2 3.6 %collective-permute-start.5 = (bf16[8,256,384]{2,1,0:T(8,128)(2,1)}, bf16[8,256,384]{2,1,0:T(8,128)(2,1)S(1)}, u32[]{:S(2)}, u32[]{:S(2)}) collective-permute-start(bf16[8,256,384]{2,1,0:T(8,128)(2,1)} %copy-done.12), channel_id=1, source_target_pairs={{0,1},{1,0},{2,3},{3,2},{4,5},{5,4},{6,7},{7,6},{8,9},{9,8},{10,11... | collective-permute-start | bytes 4718600 | tf_op jit(solution)/shard_map/ppermute | solution.py:61
  135.8 26.9 %all-to-all-start.6 = ((bf16[8,256,384]{2,1,0:T(8,128)(2,1)}), bf16[8,256,384]{2,1,0:T(8,128)(2,1)S(1)}, u32[]{:S(2)}, u32[]{:S(2)}) async-start(bf16[8,256,384]{2,1,0:T(8,128)(2,1)} %add_convert_fusion), calls=%async_computation.6 | async-start | bytes 3145728 | tf_op jit(solution)/shard_map/all_to_all | solution.py:372
  163.8 1.1 copy-start
  164.9 26.8 %all-to-all-start.7 = ((bf16[8,224,384]{2,1,0:T(8,128)(2,1)}), bf16[8,224,384]{2,1,0:T(8,128)(2,1)S(1)}, u32[]{:S(2)}, u32[]{:S(2)}) async-start(bf16[8,224,384]{2,1,0:T(8,128)(2,1)} %copy-done), calls=%async_computation.7 | async-start | bytes 2752512 | tf_op jit(solution)/shard_map/all_to_all | solution.py:384
  191.7 1.3 copy-start.2

commit v3 on v2

--- a/solution.py
+++ b/solution.py
@@ -92,8 +92,8 @@
 
 
 def feed_kernel(
-    core_ref, near_ref, far_ref, cot_near_ref, cot_far_ref, in_ref, out_ref, kept_ref, given_ref,
-    in_buf, out_buf, rows_buf, cot_buf, hidden_buf, delta_buf, in_sem, out_sem,
+    core_ref, near_ref, far_ref, back_ref, in_ref, out_ref, kept_ref, given_ref,
+    in_buf, out_buf, rows_buf, hidden_buf, delta_buf, in_sem, out_sem,
 ):
     own = pl.multiple_of(core_ref[0] * HALF, HALF)
     other = pl.multiple_of(HALF - core_ref[0] * HALF, HALF)
@@ -112,29 +112,19 @@
         out_copies.append(
             pltpu.make_async_copy(out_ref.at[:, columns], out_buf.at[:, columns], out_sem.at[step])
         )
-    for step in range(WEIGHT_COPIES):
-        out_copies[step].start()
-        in_copies[step].start()
+    for copy in in_copies + out_copies:
+        copy.start()
     rows_buf[pl.ds(own, HALF), :] = near_ref[...]
     rows_buf[pl.ds(other, HALF), :] = far_ref[...]
-    for step in range(steps):
-        for half in range(2):
-            lanes = pl.ds(half * width, width)
-            close, away = cot_near_ref[step, :, lanes], cot_far_ref[step, :, lanes]
-            rows = pl.ds(half * HALF, HALF)
-            cot_buf[rows, pl.ds(step * CHUNK, width)] = jnp.where(first_core, close, away)
-            cot_buf[rows, pl.ds(step * CHUNK + width, width)] = jnp.where(first_core, away, close)
-    pre_act, back = 0.0, 0.0
+    pre_act = 0.0
     depth = in_buf.shape[0] // WEIGHT_COPIES
     for step in range(WEIGHT_COPIES):
         span = pl.ds(step * depth, depth)
-        out_copies[step].wait()
-        back = back + dot(cot_buf[:, span], out_buf[:, span], CONTRACT_LAST)
         in_copies[step].wait()
         pre_act = pre_act + dot(rows_buf[:, span], in_buf[span, :])
     gelu_out, gelu_slope = gelu_pair(pre_act)
     hidden_buf[...] = gelu_out.astype(BF16)
-    delta_buf[...] = (back * gelu_slope).astype(BF16)
+    delta_buf[...] = (back_ref[...] * gelu_slope).astype(BF16)
 
     def store(step, place, value):
         left, right = value[:, :width], value[:, width:]
@@ -145,12 +135,14 @@
     for step in range(steps):
         columns = pl.ds(step * CHUNK, CHUNK)
         store(step, GROUP, dot(delta_buf[...], in_buf[columns, :], CONTRACT_LAST))
+    for copy in out_copies:
+        copy.wait()
     for step in range(steps):
         columns = pl.ds(step * CHUNK, CHUNK)
         store(step, 0, dot(hidden_buf[...], out_buf[:, columns]))
 
 
-def feed_forward(core, near, far, cot_near, cot_far, in_weight, out_weight):
+def feed_forward(core, near, far, back, in_weight, out_weight):
     vmem = pl.BlockSpec(memory_space=pltpu.VMEM)
     anywhere = pl.BlockSpec(memory_space=pl.ANY)
     steps = in_weight.shape[0] // CHUNK
@@ -158,13 +150,12 @@
     part = jax.ShapeDtypeStruct((steps, 2 * GROUP, CHUNK // 2), BF16)
     return pl.pallas_call(
         feed_kernel,
-        in_specs=[pl.BlockSpec(memory_space=pltpu.SMEM)] + [vmem] * 4 + [anywhere] * 2,
+        in_specs=[pl.BlockSpec(memory_space=pltpu.SMEM)] + [vmem] * 3 + [anywhere] * 2,
         out_specs=[vmem, vmem],
         out_shape=[part, part],
         scratch_shapes=[
             pltpu.VMEM(in_weight.shape, BF16),
             pltpu.VMEM(out_weight.shape, BF16),
-            pltpu.VMEM((GROUP, steps * CHUNK), BF16),
             pltpu.VMEM((GROUP, steps * CHUNK), BF16),
             pltpu.VMEM((GROUP, hidden), BF16),
             pltpu.VMEM((GROUP, hidden), BF16),
@@ -174,7 +165,51 @@
         compiler_params=pltpu.CompilerParams(vmem_limit_bytes=46 << 20),
         cost_estimate=pl.CostEstimate(flops=1 << 20, bytes_accessed=1 << 16, transcendentals=0),
         name="feed_forward",
-    )(core, near, far, cot_near, cot_far, in_weight, out_weight)
+    )(core, near, far, back, in_weight, out_weight)
+
+
+def back_kernel(core_ref, near_ref, far_ref, out_ref, back_ref, out_buf, rows_buf, sem):
+    first_core = core_ref[0] == 0
+    width = CHUNK // 2
+    copies = []
+    for chip in range(N_CHIP):
+        columns = pl.ds(chip * CHUNK, CHUNK)
+        copies.append(
+            pltpu.make_async_copy(out_ref.at[:, columns], out_buf.at[:, columns], sem.at[chip])
+        )
+        copies[-1].start()
+    total = 0.0
+    for chip in range(N_CHIP):
+        columns = pl.ds(chip * CHUNK, CHUNK)
+        for half in range(2):
+            lanes = pl.ds(half * width, width)
+            close, away = near_ref[chip, :, lanes], far_ref[chip, :, lanes]
+            rows = pl.ds(half * HALF, HALF)
+            rows_buf[rows, pl.ds(chip * CHUNK, width)] = jnp.where(first_core, close, away)
+            rows_buf[rows, pl.ds(chip * CHUNK + width, width)] = jnp.where(first_core, away, close)
+        copies[chip].wait()
+        total = total + dot(rows_buf[:, columns], out_buf[:, columns], CONTRACT_LAST)
+    back_ref[...] = total
+
+
+def back_terms(core, near, far, out_weight):
+    vmem = pl.BlockSpec(memory_space=pltpu.VMEM)
+    hidden = out_weight.shape[0]
+    return pl.pallas_call(
+        back_kernel,
+        in_specs=[pl.BlockSpec(memory_space=pltpu.SMEM), vmem, vmem]
+        + [pl.BlockSpec(memory_space=pl.ANY)],
+        out_specs=vmem,
+        out_shape=jax.ShapeDtypeStruct((GROUP, hidden), F32),
+        scratch_shapes=[
+            pltpu.VMEM(out_weight.shape, BF16),
+            pltpu.VMEM((GROUP, out_weight.shape[1]), BF16),
+            pltpu.SemaphoreType.DMA((N_CHIP,)),
+        ],
+        compiler_params=pltpu.CompilerParams(vmem_limit_bytes=46 << 20),
+        cost_estimate=pl.CostEstimate(flops=1 << 20, bytes_accessed=1 << 16, transcendentals=0),
+        name="back_terms",
+    )(core, near, far, out_weight)
 
 
 def rank_spans(lengths_ref):
@@ -327,28 +362,35 @@
     pair_matrix = jnp.concatenate([own_high, far_high], axis=1)
     partial_white = dot(all_tokens.reshape(ROWS // 2, CHUNK), pair_matrix, CONTRACT_LAST)
 
-    got = lax.all_to_all(
-        partial_white.astype(BF16).reshape(N_CHIP, HALF, CHUNK), CHIPS, 0, 0, tiled=True
-    )
-    white_chunk = jnp.sum(got.astype(F32), axis=0).astype(BF16).reshape(N_DP, PART, CHUNK)
+    sent = jnp.concatenate(
+        [
+            partial_white.astype(BF16).reshape(N_CHIP, HALF, CHUNK),
+            jnp.broadcast_to(cot_packed[None], (N_CHIP,) + cot_packed.shape),
+        ],
+        axis=1,
+    )
+    got = lax.all_to_all(sent, CHIPS, 0, 0, tiled=True)
+    cot_near = got[:, HALF:]
+    back_hidden = back_terms(core_list, cot_near, swap_core(cot_near), out_weight)
+    white_chunk = jnp.sum(got[:, :HALF].astype(F32), axis=0).astype(BF16).reshape(N_DP, PART, CHUNK)
 
     white_part = lax.all_to_all(white_chunk, DP, 0, 0, tiled=True)
 
     sent = jnp.concatenate(
-        [white_part.reshape(HALF, CHUNK), white_chunk.reshape(HALF, CHUNK), cot_packed], axis=0
+        [white_part.reshape(HALF, CHUNK), white_chunk.reshape(HALF, CHUNK)], axis=0
     )
     sent = jnp.broadcast_to(sent[None], (N_CHIP,) + sent.shape)
     got = lax.all_to_all(sent, CHIPS, 0, 0, tiled=True)
+
+    got = lax.optimization_barrier((got, back_hidden))[0]
 
     def wide_rows(block):
         block = block.reshape(N_CHIP, N_DP, PART, CHUNK)
         return jnp.transpose(block, (0, 2, 1, 3)).reshape(HALF, N_DP * CHUNK)
 
-    decor_near = wide_rows(got[:, HALF : 2 * HALF])
-    cot_near = got[:, 2 * HALF :]
+    decor_near = wide_rows(got[:, HALF:])
     feed_near = wide_rows(got[:, :HALF])
     decor_far = swap_core(decor_near)
-    cot_far = swap_core(cot_near)
     feed_far = swap_core(feed_near)
 
     group_row = jnp.arange(GROUP, dtype=jnp.int32) * N_DP
@@ -365,7 +407,7 @@
     feed_near = lax.optimization_barrier((feed_near, mixed_part))[0]
 
     kept, given = feed_forward(
-        core_list, feed_near, feed_far, cot_near, cot_far, in_weight, out_weight
+        core_list, feed_near, feed_far, back_hidden, in_weight, out_weight
     )
     given = lax.optimization_barrier((given, mixed_got))[0]
     summed = (kept.astype(F32) + swap_core(given).astype(F32)).astype(BF16)

time: 197 us -> 195 us (0.990)
  blocking collectives: 75 us -> 52.1 us
  waiting for transfers between devices: 57.2 us -> 67.5 us
  starting transfers between devices: 21.4 us -> 26.8 us
  local copies, waits for them, and re-layouts: 9.73 us -> 12.3 us
    all_to_all x1 -> x0, blocking collectives: 19 us -> none  [local(): lax.all_to_all(partial_white.astype(BF16).reshape(N_CHIP, HALF, CHUNK), C...]
    all_to_all x0 -> x1, waiting for transfers between devices: none -> 8.47 us  [local(): got = lax.all_to_all(sent, CHIPS, 0, 0, tiled=True)]
    all_to_all x0 -> x1, starting transfers between devices: none -> 6.75 us  [local(): got = lax.all_to_all(sent, CHIPS, 0, 0, tiled=True)]
    pallas_call x0 -> x1, Pallas kernels: none -> 6.23 us  [back_terms(): pl.pallas_call(back_kernel, in_specs=[pl.BlockSpec(memory_space=pltpu.SME...]
    pallas_call x1, Pallas kernels: 15.6 us -> 11.2 us  [feed_forward(): pl.pallas_call(feed_kernel, in_specs=[pl.BlockSpec(memory_space=pltpu.SME...]
    all_to_all x1, blocking collectives: 31.4 us -> 27.4 us  [local(): got = lax.all_to_all(sent, CHIPS, 0, 0, tiled=True)]
    ppermute x6, waiting for transfers between devices: 6.59 us -> 8.76 us  [swap_core(): return lax.ppermute(value, CORE, [(0, 1), (1, 0)])]
  transfers between devices with their start and end apart: 10 -> 11, of which waited for: 6 -> 8; matrix products, arithmetic and copies ran while one was open for 2% -> 2% of each run, Pallas kernels for 9% -> 10%
where the time goes in v3:
time: 195 us; the launch traced here: 194 us
  waiting for transfers between devices  67.5 us (35%)
  blocking collectives  52.1 us (27%)
  Pallas kernels  26.8 us (14%)
  starting transfers between devices  26.8 us (14%)
  local copies, waits for them, and re-layouts  12.3 us (6%)
  other arithmetic  6.54 us (3%)
    all_to_all x2, waiting for transfers between devices, local(): got = lax.all_to_all(sent, DP, 0, 0, tiled=True)  31.9 us
    all_to_all x1, blocking collectives, local(): got = lax.all_to_all(sent, CHIPS, 0, 0, tiled=True)  27.4 us
    all_to_all x1, waiting for transfers between devices, local(): got = lax.all_to_all(summed, CHIPS, 0, 0, tiled=True)  18.3 us
    all_to_all x1, blocking collectives, local(): got = lax.all_to_all(sent, DP, 0, 0, tiled=True)  15.6 us
    pallas_call x1, Pallas kernels, feed_forward(): pl.pallas_call(feed_kernel, in_specs=[pl.BlockSpec(memory_space=pltpu.SME...  11.2 us
    all_to_all x1, blocking collectives, local(): white_part = lax.all_to_all(white_chunk, DP, 0, 0, tiled=True)  9.04 us
    all_to_all x2, starting transfers between devices, local(): got = lax.all_to_all(sent, DP, 0, 0, tiled=True)  9.03 us
    ppermute x6, waiting for transfers between devices, swap_core(): return lax.ppermute(value, CORE, [(0, 1), (1, 0)])  8.76 us
  transfers between devices with their start and end apart: 11, of which 8 were waited for; matrix products, arithmetic and copies ran while one was open for 2% of the time, Pallas kernels for 10%

profile of v3, /device:TPU:16, one launch (start us, length us, event | category | flops | bytes accessed | tf_op | source)
XLA Modules:
  0.0 193.8 jit_solution(865836007235818003)
XLA Ops:
  0.6 0.0 copy-start.11
  0.6 0.1 pad_add_fusion.place_ref
  0.7 0.9 copy-done.8
  1.7 0.9 copy-done.9
  2.6 0.7 copy-done.10
  3.3 1.4 pack_kernel.1
  4.7 15.6 %all_to_all.40.got_ref = bf16[8,48,768]{2,1,0:T(8,128)(2,1)S(1)} all-to-all(bf16[8,48,768]{2,1,0:T(8,128)(2,1)S(1)} %pack_kernel.1), channel_id=1, replica_groups=mesh['x'=4,'yl'=2,'yh'=2,'z'=4,'core'=2] {'x','yl'}, dimensions={0} | all-to-all | bytes 1179648 | tf_op jit(solution)/shard_map/all_to_all | solution.py:344
  20.4 0.0 copy-done.11
  20.4 1.2 group_kernel.1
  21.6 0.1 collective-permute-start
  21.7 1.2 collective-permute-done
  22.9 0.9 broadcast_in_dim.28
  23.9 3.5 %all-to-all-start.1 = ((bf16[8,64,768]{2,1,0:T(8,128)(2,1)}), bf16[8,64,768]{2,1,0:T(8,128)(2,1)S(1)}, u32[]{:S(2)}, u32[]{:S(2)}) async-start(bf16[8,64,768]{2,1,0:T(8,128)(2,1)} %broadcast_in_dim.28), calls=%async_computation.1 | async-start | bytes 1572864 | tf_op jit(solution)/shard_map/all_to_all | solution.py:357
  27.4 1.0 fusion.1
  28.4 0.2 collective-permute-start.1
  28.6 12.1 %all-to-all-done.1 = bf16[8,64,768]{2,1,0:T(8,128)(2,1)S(1)} async-done(((bf16[8,64,768]{2,1,0:T(8,128)(2,1)}), bf16[8,64,768]{2,1,0:T(8,128)(2,1)S(1)}, u32[]{:S(2)}, u32[]{:S(2)}) %all-to-all-start.1) | async-done | bytes 786464 | tf_op jit(solution)/shard_map/all_to_all | solution.py:357
  40.7 0.1 copy.15
  40.8 0.0 collective-permute-done.1
  40.8 0.8 convolution_convert_fusion
  41.6 0.1 broadcast_in_dim.29
  41.7 0.1 pad_maximum_fusion
  41.8 27.4 %all_to_all.41 = bf16[8,128,768]{2,1,0:T(8,128)(2,1)S(1)} all-to-all(bf16[8,128,768]{2,1,0:T(8,128)(2,1)S(1)} %pad_maximum_fusion), channel_id=1, replica_groups=mesh['x'=4,'yl'=2,'yh'=2,'z'=4,'core'=2] {'yh','z'}, dimensions={0} | all-to-all | bytes 3145728 | tf_op jit(solution)/shard_map/all_to_all | solution.py:372
  69.2 0.1 fusion.7
  69.3 9.0 %all_to_all.42 = bf16[8,8,768]{2,1,0:T(8,128)(2,1)S(1)} all-to-all(bf16[8,8,768]{2,1,0:T(8,128)(2,1)S(1)} %bitcast.30), channel_id=1, replica_groups=mesh['x'=4,'yl'=2,'yh'=2,'z'=4,'core'=2] {'x','yl'}, dimensions={0} | all-to-all | bytes 196608 | tf_op jit(solution)/shard_map/all_to_all | solution.py:377
  78.4 1.2 broadcast_in_dim.30
  79.6 6.8 %all-to-all-start.4 = ((bf16[8,128,768]{2,1,0:T(8,128)(2,1)}), bf16[8,128,768]{2,1,0:T(8,128)(2,1)}, u32[]{:S(2)}, u32[]{:S(2)}) async-start(bf16[8,128,768]{2,1,0:T(8,128)(2,1)} %broadcast_in_dim.30), calls=%async_computation.4 | async-start | bytes 3145728 | tf_op jit(solution)/shard_map/all_to_all | solution.py:383
  86.4 0.0 collective-permute-start.2
  86.4 2.3 %collective-permute-done.2.far_ref = bf16[8,64,768]{2,1,0:T(8,128)(2,1)S(1)} collective-permute-done((bf16[8,64,768]{2,1,0:T(8,128)(2,1)S(1)}, bf16[8,64,768]{2,1,0:T(8,128)(2,1)S(1)}, u32[]{:S(2)}, u32[]{:S(2)}) %collective-permute-start.2) | collective-permute-done | bytes 786464 | tf_op jit(solution)/shard_map/ppermute | solution.py:61
  88.7 6.2 %back_terms.1.back_ref = f32[128,768]{1,0:T(8,128)S(1)} custom-call(s32[1]{0:T(128)} %bitcast.1.core_ref, bf16[8,64,768]{2,1,0:T(8,128)(2,1)S(1)} %get-tuple-element.25.near_ref, bf16[8,64,768]{2,1,0:T(8,128)(2,1)S(1)} %collective-permute-done.2.far_ref, bf16[768,6144]{1,0:T(8,128)(2,1)} %out_ref.3), custom_call_target="tpu_custom_call" | custom-call | flops 1048576 | bytes 65536 | tf_op jit(solution)/shard_map/back_terms/pallas_call | solution.py:198
  94.9 8.5 %all-to-all-done.4 = bf16[8,128,768]{2,1,0:T(8,128)(2,1)} async-done(((bf16[8,128,768]{2,1,0:T(8,128)(2,1)}), bf16[8,128,768]{2,1,0:T(8,128)(2,1)}, u32[]{:S(2)}, u32[]{:S(2)}) %all-to-all-start.4) | async-done | bytes 1572896 | tf_op jit(solution)/shard_map/all_to_all | solution.py:383
  103.4 1.6 fusion.6
  105.0 0.1 collective-permute-start.3
  105.0 0.5 collective-permute-start.4
  105.5 1.8 collective-permute-done.3.far_ref
  107.3 1.9 mixed_terms.1
  109.2 0.0 copy-start.4
  109.2 0.9 copy-done.4
  110.1 4.4 %all-to-all-start.5 = ((bf16[8,128,384]{2,1,0:T(8,128)(2,1)}), bf16[8,128,384]{2,1,0:T(8,128)(2,1)}, u32[]{:S(2)}, u32[]{:S(2)}) async-start(bf16[8,128,384]{2,1,0:T(8,128)(2,1)} %copy-done.4), calls=%async_computation.5 | async-start | bytes 1572864 | tf_op jit(solution)/shard_map/all_to_all | solution.py:402
  114.5 0.0 collective-permute-done.4.far_ref
  114.5 11.2 %feed_forward.1 = (bf16[8,256,384]{2,1,0:T(8,128)(2,1)S(1)}, bf16[8,256,384]{2,1,0:T(8,128)(2,1)S(1)}) custom-call(s32[1]{0:T(128)} %bitcast.1.core_ref, bf16[64,6144]{1,0:T(8,128)(2,1)S(1)} %bitcast.26, bf16[64,6144]{1,0:T(8,128)(2,1)S(1)} %collective-permute-done.4.far_ref, f32[128,768]{1,0:T(8,128)S(1)} %back_terms.1.back_ref, bf16[6144,768]{1,0:T(8,128)(2,1)} %in_ref.1, ...), custom_call_target="tpu_custom_call" | custom-call | flops 1048576 | bytes 65536 | tf_op jit(solution)/shard_map/feed_forward/pallas_call | solution.py:151
  125.7 1.2 copy-done.3
  126.9 1.1 copy-done.12
  128.0 0.0 all-to-all-done.5
  128.0 0.1 collective-permute-start.5
  128.2 3.5 %collective-permute-done.5 = bf16[8,256,384]{2,1,0:T(8,128)(2,1)S(1)} collective-permute-done((bf16[8,256,384]{2,1,0:T(8,128)(2,1)}, bf16[8,256,384]{2,1,0:T(8,128)(2,1)S(1)}, u32[]{:S(2)}, u32[]{:S(2)}) %collective-permute-start.5) | collective-permute-done | bytes 1572896 | tf_op jit(solution)/shard_map/ppermute | solution.py:61
  131.7 2.9 %add_convert_fusion = bf16[8,256,384]{2,1,0:T(8,128)(2,1)} fusion(bf16[8,256,384]{2,1,0:T(8,128)(2,1)S(1)} %collective-permute-done.5, bf16[8,256,384]{2,1,0:T(8,128)(2,1)} %copy-done.3), kind=kLoop, calls=%fused_computation.2 | loop fusion | flops 3145728 | bytes 4718592 | tf_op jit(solution)/shard_map/convert_element_type | solution.py:413
  134.6 5.7 %all-to-all-start.6 = ((bf16[8,256,384]{2,1,0:T(8,128)(2,1)}), bf16[8,256,384]{2,1,0:T(8,128)(2,1)S(1)}, u32[]{:S(2)}, u32[]{:S(2)}) async-start(bf16[8,256,384]{2,1,0:T(8,128)(2,1)} %add_convert_fusion), calls=%async_computation.6 | async-start | bytes 3145728 | tf_op jit(solution)/shard_map/all_to_all | solution.py:414
  140.2 0.1 reshape.122
  140.3 0.1 reshape.120
  140.4 0.1 reduce-window.7
  140.5 0.1 reduce.2
  140.6 0.1 select_reduce_fusion.1
  140.8 1.3 convert_reduce_fusion
  142.0 0.1 multiply_convert_fusion.mixed_ref
  142.1 18.3 %all-to-all-done.6.got_ref = bf16[8,256,384]{2,1,0:T(8,128)(2,1)S(1)} async-done(((bf16[8,256,384]{2,1,0:T(8,128)(2,1)}), bf16[8,256,384]{2,1,0:T(8,128)(2,1)S(1)}, u32[]{:S(2)}, u32[]{:S(2)}) %all-to-all-start.6) | async-done | bytes 1572896 | tf_op jit(solution)/shard_map/all_to_all | solution.py:414
  160.4 1.2 spread_kernel.1
  161.6 1.1 copy-done
  162.7 5.5 %all-to-all-start.7 = ((bf16[8,224,384]{2,1,0:T(8,128)(2,1)}), bf16[8,224,384]{2,1,0:T(8,128)(2,1)S(1)}, u32[]{:S(2)}, u32[]{:S(2)}) async-start(bf16[8,224,384]{2,1,0:T(8,128)(2,1)} %copy-done), calls=%async_computation.7 | async-start | bytes 2752512 | tf_op jit(solution)/shard_map/all_to_all | solution.py:426
  168.2 0.1 select_reduce_fusion
  168.4 0.5 fusion
  168.9 0.2 broadcast_in_dim.40.diagonal_ref
  169.0 19.8 %all-to-all-done.7.got_ref = bf16[8,224,384]{2,1,0:T(8,128)(2,1)S(1)} async-done(((bf16[8,224,384]{2,1,0:T(8,128)(2,1)}), bf16[8,224,384]{2,1,0:T(8,128)(2,1)S(1)}, u32[]{:S(2)}, u32[]{:S(2)}) %all-to-all-start.7) | async-done | bytes 1376288 | tf_op jit(solution)/shard_map/all_to_all | solution.py:426
  188.9 1.3 copy-done.2
  190.1 3.6 %final_kernel.1 = (bf16[320,384]{1,0:T(8,128)(2,1)}, bf16[320,384]{1,0:T(8,128)(2,1)}, f32[768,384]{1,0:T(8,128)}) custom-call(s32[2]{0:T(128)S(1)} %pad_add_fusion.place_ref, s32[8,8]{1,0:T(8,128)S(1)} %copy-done.11, bf16[8,224,384]{2,1,0:T(8,128)(2,1)S(1)} %all-to-all-done.7.got_ref, bf16[1024,768]{1,0:T(8,128)(2,1)S(1)} %bitcast.24, ...), custom_call_target="tpu_custom_call" | custom-call | flops 1048576 | bytes 65536 | tf_op jit(solution)/shard_map/final_kernel/pallas_call | solution.py:319
  (22 shorter events, 0.1 us)
Async XLA Ops:
  0.6 19.8 %copy-start.11 = (s32[8,8]{1,0:T(8,128)S(1)}, s32[8,8]{1,0:T(8,128)}, u32[]{:S(2)}) copy-start(s32[8,8]{1,0:T(8,128)} %lengths_ref.7) | copy-start | bytes 772
  0.7 0.9 copy-start.8
  1.7 0.9 copy-start.9
  2.6 0.7 copy-start.10
  20.4 7.0 %copy-start.1 = (f32[768,384]{1,0:T(8,128)S(1)}, f32[768,384]{1,0:T(8,128)}, u32[]{:S(2)}) copy-start(f32[768,384]{1,0:T(8,128)} %matrix_ref.1) | copy-start | bytes 3538948
  21.6 1.3 collective-permute-start
  23.9 16.9 %all-to-all-start.1 = ((bf16[8,64,768]{2,1,0:T(8,128)(2,1)}), bf16[8,64,768]{2,1,0:T(8,128)(2,1)S(1)}, u32[]{:S(2)}, u32[]{:S(2)}) async-start(bf16[8,64,768]{2,1,0:T(8,128)(2,1)} %broadcast_in_dim.28), calls=%async_computation.1 | async-start | bytes 1572864 | tf_op jit(solution)/shard_map/all_to_all | solution.py:357
  28.4 13.2 %copy-start.6 = (bf16[768,384]{1,0:T(8,128)(2,1)}, bf16[768,384]{1,0:T(8,128)(2,1)S(1)}, u32[]{:S(2)}) copy-start(bf16[768,384]{1,0:T(8,128)(2,1)S(1)} %get-tuple-element.28.high_ref) | copy-start | bytes 1769476
  28.4 12.3 %collective-permute-start.1 = (bf16[768,384]{1,0:T(8,128)(2,1)S(1)}, bf16[768,384]{1,0:T(8,128)(2,1)S(1)}, u32[]{:S(2)}, u32[]{:S(2)}) collective-permute-start(bf16[768,384]{1,0:T(8,128)(2,1)S(1)} %get-tuple-element.28.high_ref), channel_id=1, source_target_pairs={{0,1},{1,0},{2,3},{3,2},{4,5},{5,4},{6,7},{7,6},{8,9},{9,8},{10,11... | collective-permute-start | bytes 1769480 | tf_op jit(solution)/shard_map/ppermute | solution.py:61
  79.6 23.7 %all-to-all-start.4 = ((bf16[8,128,768]{2,1,0:T(8,128)(2,1)}), bf16[8,128,768]{2,1,0:T(8,128)(2,1)}, u32[]{:S(2)}, u32[]{:S(2)}) async-start(bf16[8,128,768]{2,1,0:T(8,128)(2,1)} %broadcast_in_dim.30), calls=%async_computation.4 | async-start | bytes 3145728 | tf_op jit(solution)/shard_map/all_to_all | solution.py:383
  86.4 2.3 %collective-permute-start.2 = (bf16[8,64,768]{2,1,0:T(8,128)(2,1)S(1)}, bf16[8,64,768]{2,1,0:T(8,128)(2,1)S(1)}, u32[]{:S(2)}, u32[]{:S(2)}) collective-permute-start(bf16[8,64,768]{2,1,0:T(8,128)(2,1)S(1)} %get-tuple-element.25.near_ref), channel_id=1, source_target_pairs={{0,1},{1,0},{2,3},{3,2},{4,5},{5,4},{6,7},{7,6},{8,9},{9,8},{10,11... | collective-permute-start | bytes 2359304 | tf_op jit(solution)/shard_map/ppermute | solution.py:61
  103.4 4.0 %copy-start.5 = (bf16[768,384]{1,0:T(8,128)(2,1)S(1)}, bf16[768,384]{1,0:T(8,128)(2,1)}, u32[]{:S(2)}) copy-start(bf16[768,384]{1,0:T(8,128)(2,1)} %get-tuple-element.27.low_ref) | copy-start | bytes 1769476
  103.4 4.0 %copy-start.7 = (bf16[768,384]{1,0:T(8,128)(2,1)S(1)}, bf16[768,384]{1,0:T(8,128)(2,1)}, u32[]{:S(2)}) copy-start(bf16[768,384]{1,0:T(8,128)(2,1)} %copy-done.6) | copy-start | bytes 1769476
  105.0 2.4 %collective-permute-start.3 = (bf16[64,6144]{1,0:T(8,128)(2,1)S(1)}, bf16[64,6144]{1,0:T(8,128)(2,1)S(1)}, u32[]{:S(2)}, u32[]{:S(2)}) collective-permute-start(bf16[64,6144]{1,0:T(8,128)(2,1)S(1)} %bitcast.27), channel_id=1, source_target_pairs={{0,1},{1,0},{2,3},{3,2},{4,5},{5,4},{6,7},{7,6},{8,9},{9,8},{10,11... | collective-permute-start | bytes 2359304 | tf_op jit(solution)/shard_map/ppermute | solution.py:61
  105.0 9.4 %collective-permute-start.4 = (bf16[64,6144]{1,0:T(8,128)(2,1)S(1)}, bf16[64,6144]{1,0:T(8,128)(2,1)S(1)}, u32[]{:S(2)}, u32[]{:S(2)}) collective-permute-start(bf16[64,6144]{1,0:T(8,128)(2,1)S(1)} %bitcast.25), channel_id=1, source_target_pairs={{0,1},{1,0},{2,3},{3,2},{4,5},{5,4},{6,7},{7,6},{8,9},{9,8},{10,11... | collective-permute-start | bytes 2359304 | tf_op jit(solution)/shard_map/ppermute | solution.py:61
  109.2 0.9 copy-start.4
  110.1 18.0 %all-to-all-start.5 = ((bf16[8,128,384]{2,1,0:T(8,128)(2,1)}), bf16[8,128,384]{2,1,0:T(8,128)(2,1)}, u32[]{:S(2)}, u32[]{:S(2)}) async-start(bf16[8,128,384]{2,1,0:T(8,128)(2,1)} %copy-done.4), calls=%async_computation.5 | async-start | bytes 1572864 | tf_op jit(solution)/shard_map/all_to_all | solution.py:402
  125.7 1.2 copy-start.3
  126.9 1.1 copy-start.12
  128.0 3.6 %collective-permute-start.5 = (bf16[8,256,384]{2,1,0:T(8,128)(2,1)}, bf16[8,256,384]{2,1,0:T(8,128)(2,1)S(1)}, u32[]{:S(2)}, u32[]{:S(2)}) collective-permute-start(bf16[8,256,384]{2,1,0:T(8,128)(2,1)} %copy-done.12), channel_id=1, source_target_pairs={{0,1},{1,0},{2,3},{3,2},{4,5},{5,4},{6,7},{7,6},{8,9},{9,8},{10,11... | collective-permute-start | bytes 4718600 | tf_op jit(solution)/shard_map/ppermute | solution.py:61
  134.6 25.8 %all-to-all-start.6 = ((bf16[8,256,384]{2,1,0:T(8,128)(2,1)}), bf16[8,256,384]{2,1,0:T(8,128)(2,1)S(1)}, u32[]{:S(2)}, u32[]{:S(2)}) async-start(bf16[8,256,384]{2,1,0:T(8,128)(2,1)} %add_convert_fusion), calls=%async_computation.6 | async-start | bytes 3145728 | tf_op jit(solution)/shard_map/all_to_all | solution.py:414
  161.6 1.1 copy-start
  162.7 26.1 %all-to-all-start.7 = ((bf16[8,224,384]{2,1,0:T(8,128)(2,1)}), bf16[8,224,384]{2,1,0:T(8,128)(2,1)S(1)}, u32[]{:S(2)}, u32[]{:S(2)}) async-start(bf16[8,224,384]{2,1,0:T(8,128)(2,1)} %copy-done), calls=%async_computation.7 | async-start | bytes 2752512 | tf_op jit(solution)/shard_map/all_to_all | solution.py:426
  188.9 1.3 copy-start.2

commit v4 on v3

--- a/solution.py
+++ b/solution.py
@@ -112,7 +112,7 @@
         out_copies.append(
             pltpu.make_async_copy(out_ref.at[:, columns], out_buf.at[:, columns], out_sem.at[step])
         )
-    for copy in in_copies + out_copies:
+    for copy in in_copies:
         copy.start()
     rows_buf[pl.ds(own, HALF), :] = near_ref[...]
     rows_buf[pl.ds(other, HALF), :] = far_ref[...]
@@ -121,6 +121,7 @@
     for step in range(WEIGHT_COPIES):
         span = pl.ds(step * depth, depth)
         in_copies[step].wait()
+        out_copies[step].start()
         pre_act = pre_act + dot(rows_buf[:, span], in_buf[span, :])
     gelu_out, gelu_slope = gelu_pair(pre_act)
     hidden_buf[...] = gelu_out.astype(BF16)

time: 195 us -> 193 us (0.990)
  Pallas kernels: 26.8 us -> 24.8 us
    pallas_call x1, Pallas kernels: 11.2 us -> 9.19 us  [feed_forward(): pl.pallas_call(feed_kernel, in_specs=[pl.BlockSpec(memory_space=pltpu.SME...]
  transfers between devices with their start and end apart: 11 -> 11, of which waited for: 8 -> 9; matrix products, arithmetic and copies ran while one was open for 2% -> 2% of each run, Pallas kernels for 10% -> 9%
where the time goes in v4:
time: 193 us; the launch traced here: 192 us
  waiting for transfers between devices  69.4 us (36%)
  blocking collectives  52.1 us (27%)
  starting transfers between devices  25 us (13%)
  Pallas kernels  24.8 us (13%)
  local copies, waits for them, and re-layouts  12.3 us (6%)
  other arithmetic  6.54 us (3%)
    all_to_all x2, waiting for transfers between devices, local(): got = lax.all_to_all(sent, DP, 0, 0, tiled=True)  32 us
    all_to_all x1, blocking collectives, local(): got = lax.all_to_all(sent, CHIPS, 0, 0, tiled=True)  27.4 us
    all_to_all x1, waiting for transfers between devices, local(): got = lax.all_to_all(summed, CHIPS, 0, 0, tiled=True)  18.3 us
    all_to_all x1, blocking collectives, local(): got = lax.all_to_all(sent, DP, 0, 0, tiled=True)  15.6 us
    pallas_call x1, Pallas kernels, feed_forward(): pl.pallas_call(feed_kernel, in_specs=[pl.BlockSpec(memory_space=pltpu.SME...  9.19 us
    all_to_all x1, blocking collectives, local(): white_part = lax.all_to_all(white_chunk, DP, 0, 0, tiled=True)  9.04 us
    ppermute x6, waiting for transfers between devices, swap_core(): return lax.ppermute(value, CORE, [(0, 1), (1, 0)])  8.9 us
    all_to_all x1, waiting for transfers between devices, local(): got = lax.all_to_all(sent, CHIPS, 0, 0, tiled=True)  8.47 us
  transfers between devices with their start and end apart: 11, of which 9 were waited for; matrix products, arithmetic and copies ran while one was open for 2% of the time, Pallas kernels for 9%

profile of v4, /device:TPU:16, one launch (start us, length us, event | category | flops | bytes accessed | tf_op | source)
XLA Modules:
  0.0 191.8 jit_solution(14134420479594546846)
XLA Ops:
  0.6 0.0 copy-start.11
  0.6 0.1 pad_add_fusion.place_ref
  0.7 0.9 copy-done.8
  1.7 0.9 copy-done.9
  2.6 0.7 copy-done.10
  3.3 1.4 pack_kernel.1
  4.7 15.6 %all_to_all.40.got_ref = bf16[8,48,768]{2,1,0:T(8,128)(2,1)S(1)} all-to-all(bf16[8,48,768]{2,1,0:T(8,128)(2,1)S(1)} %pack_kernel.1), channel_id=1, replica_groups=mesh['x'=4,'yl'=2,'yh'=2,'z'=4,'core'=2] {'x','yl'}, dimensions={0} | all-to-all | bytes 1179648 | tf_op jit(solution)/shard_map/all_to_all | solution.py:345
  20.4 0.0 copy-done.11
  20.4 1.2 group_kernel.1
  21.6 0.1 collective-permute-start
  21.7 1.2 collective-permute-done
  22.9 0.9 broadcast_in_dim.28
  23.9 3.5 %all-to-all-start.1 = ((bf16[8,64,768]{2,1,0:T(8,128)(2,1)}), bf16[8,64,768]{2,1,0:T(8,128)(2,1)S(1)}, u32[]{:S(2)}, u32[]{:S(2)}) async-start(bf16[8,64,768]{2,1,0:T(8,128)(2,1)} %broadcast_in_dim.28), calls=%async_computation.1 | async-start | bytes 1572864 | tf_op jit(solution)/shard_map/all_to_all | solution.py:358
  27.4 1.0 fusion.1
  28.4 0.2 collective-permute-start.1
  28.6 12.1 %all-to-all-done.1 = bf16[8,64,768]{2,1,0:T(8,128)(2,1)S(1)} async-done(((bf16[8,64,768]{2,1,0:T(8,128)(2,1)}), bf16[8,64,768]{2,1,0:T(8,128)(2,1)S(1)}, u32[]{:S(2)}, u32[]{:S(2)}) %all-to-all-start.1) | async-done | bytes 786464 | tf_op jit(solution)/shard_map/all_to_all | solution.py:358
  40.7 0.1 copy.15
  40.8 0.0 collective-permute-done.1
  40.8 0.8 convolution_convert_fusion
  41.6 0.1 broadcast_in_dim.29
  41.7 0.1 pad_maximum_fusion
  41.8 27.4 %all_to_all.41 = bf16[8,128,768]{2,1,0:T(8,128)(2,1)S(1)} all-to-all(bf16[8,128,768]{2,1,0:T(8,128)(2,1)S(1)} %pad_maximum_fusion), channel_id=1, replica_groups=mesh['x'=4,'yl'=2,'yh'=2,'z'=4,'core'=2] {'yh','z'}, dimensions={0} | all-to-all | bytes 3145728 | tf_op jit(solution)/shard_map/all_to_all | solution.py:373
  69.2 0.1 fusion.7
  69.3 9.0 %all_to_all.42 = bf16[8,8,768]{2,1,0:T(8,128)(2,1)S(1)} all-to-all(bf16[8,8,768]{2,1,0:T(8,128)(2,1)S(1)} %bitcast.30), channel_id=1, replica_groups=mesh['x'=4,'yl'=2,'yh'=2,'z'=4,'core'=2] {'x','yl'}, dimensions={0} | all-to-all | bytes 196608 | tf_op jit(solution)/shard_map/all_to_all | solution.py:378
  78.4 1.2 broadcast_in_dim.30
  79.6 6.8 %all-to-all-start.4 = ((bf16[8,128,768]{2,1,0:T(8,128)(2,1)}), bf16[8,128,768]{2,1,0:T(8,128)(2,1)}, u32[]{:S(2)}, u32[]{:S(2)}) async-start(bf16[8,128,768]{2,1,0:T(8,128)(2,1)} %broadcast_in_dim.30), calls=%async_computation.4 | async-start | bytes 3145728 | tf_op jit(solution)/shard_map/all_to_all | solution.py:384
  86.4 0.0 collective-permute-start.2
  86.4 2.3 %collective-permute-done.2.far_ref = bf16[8,64,768]{2,1,0:T(8,128)(2,1)S(1)} collective-permute-done((bf16[8,64,768]{2,1,0:T(8,128)(2,1)S(1)}, bf16[8,64,768]{2,1,0:T(8,128)(2,1)S(1)}, u32[]{:S(2)}, u32[]{:S(2)}) %collective-permute-start.2) | collective-permute-done | bytes 786464 | tf_op jit(solution)/shard_map/ppermute | solution.py:61
  88.7 6.2 %back_terms.1.back_ref = f32[128,768]{1,0:T(8,128)S(1)} custom-call(s32[1]{0:T(128)} %bitcast.1.core_ref, bf16[8,64,768]{2,1,0:T(8,128)(2,1)S(1)} %get-tuple-element.25.near_ref, bf16[8,64,768]{2,1,0:T(8,128)(2,1)S(1)} %collective-permute-done.2.far_ref, bf16[768,6144]{1,0:T(8,128)(2,1)} %out_ref.3), custom_call_target="tpu_custom_call" | custom-call | flops 1048576 | bytes 65536 | tf_op jit(solution)/shard_map/back_terms/pallas_call | solution.py:199
  94.9 8.5 %all-to-all-done.4 = bf16[8,128,768]{2,1,0:T(8,128)(2,1)} async-done(((bf16[8,128,768]{2,1,0:T(8,128)(2,1)}), bf16[8,128,768]{2,1,0:T(8,128)(2,1)}, u32[]{:S(2)}, u32[]{:S(2)}) %all-to-all-start.4) | async-done | bytes 1572896 | tf_op jit(solution)/shard_map/all_to_all | solution.py:384
  103.4 1.6 fusion.6
  105.0 0.1 collective-permute-start.3
  105.0 0.5 collective-permute-start.4
  105.5 1.8 collective-permute-done.3.far_ref
  107.3 1.9 mixed_terms.1
  109.2 0.0 copy-start.4
  109.2 0.9 copy-done.4
  110.1 4.4 %all-to-all-start.5 = ((bf16[8,128,384]{2,1,0:T(8,128)(2,1)}), bf16[8,128,384]{2,1,0:T(8,128)(2,1)}, u32[]{:S(2)}, u32[]{:S(2)}) async-start(bf16[8,128,384]{2,1,0:T(8,128)(2,1)} %copy-done.4), calls=%async_computation.5 | async-start | bytes 1572864 | tf_op jit(solution)/shard_map/all_to_all | solution.py:403
  114.5 0.0 collective-permute-done.4.far_ref
  114.5 9.2 %feed_forward.1 = (bf16[8,256,384]{2,1,0:T(8,128)(2,1)S(1)}, bf16[8,256,384]{2,1,0:T(8,128)(2,1)S(1)}) custom-call(s32[1]{0:T(128)} %bitcast.1.core_ref, bf16[64,6144]{1,0:T(8,128)(2,1)S(1)} %bitcast.26, bf16[64,6144]{1,0:T(8,128)(2,1)S(1)} %collective-permute-done.4.far_ref, f32[128,768]{1,0:T(8,128)S(1)} %back_terms.1.back_ref, bf16[6144,768]{1,0:T(8,128)(2,1)} %in_ref.1, ...), custom_call_target="tpu_custom_call" | custom-call | flops 1048576 | bytes 65536 | tf_op jit(solution)/shard_map/feed_forward/pallas_call | solution.py:152
  123.7 1.2 copy-done.3
  124.9 1.1 copy-done.12
  126.0 1.7 all-to-all-done.5
  127.7 0.0 collective-permute-start.5
  127.7 3.6 %collective-permute-done.5 = bf16[8,256,384]{2,1,0:T(8,128)(2,1)S(1)} collective-permute-done((bf16[8,256,384]{2,1,0:T(8,128)(2,1)}, bf16[8,256,384]{2,1,0:T(8,128)(2,1)S(1)}, u32[]{:S(2)}, u32[]{:S(2)}) %collective-permute-start.5) | collective-permute-done | bytes 1572896 | tf_op jit(solution)/shard_map/ppermute | solution.py:61
  131.3 2.9 %add_convert_fusion = bf16[8,256,384]{2,1,0:T(8,128)(2,1)} fusion(bf16[8,256,384]{2,1,0:T(8,128)(2,1)S(1)} %collective-permute-done.5, bf16[8,256,384]{2,1,0:T(8,128)(2,1)} %copy-done.3), kind=kLoop, calls=%fused_computation.2 | loop fusion | flops 3145728 | bytes 4718592 | tf_op jit(solution)/shard_map/convert_element_type | solution.py:414
  134.3 5.7 %all-to-all-start.6 = ((bf16[8,256,384]{2,1,0:T(8,128)(2,1)}), bf16[8,256,384]{2,1,0:T(8,128)(2,1)S(1)}, u32[]{:S(2)}, u32[]{:S(2)}) async-start(bf16[8,256,384]{2,1,0:T(8,128)(2,1)} %add_convert_fusion), calls=%async_computation.6 | async-start | bytes 3145728 | tf_op jit(solution)/shard_map/all_to_all | solution.py:415
  139.9 0.1 reshape.122
  140.0 0.1 reshape.120
  140.1 0.1 reduce-window.7
  140.2 0.1 reduce.2
  140.3 0.1 select_reduce_fusion.1
  140.4 1.3 convert_reduce_fusion
  141.7 0.1 multiply_convert_fusion.mixed_ref
  141.8 18.3 %all-to-all-done.6.got_ref = bf16[8,256,384]{2,1,0:T(8,128)(2,1)S(1)} async-done(((bf16[8,256,384]{2,1,0:T(8,128)(2,1)}), bf16[8,256,384]{2,1,0:T(8,128)(2,1)S(1)}, u32[]{:S(2)}, u32[]{:S(2)}) %all-to-all-start.6) | async-done | bytes 1572896 | tf_op jit(solution)/shard_map/all_to_all | solution.py:415
  160.1 1.2 spread_kernel.1
  161.3 1.1 copy-done
  162.4 3.8 %all-to-all-start.7 = ((bf16[8,224,384]{2,1,0:T(8,128)(2,1)}), bf16[8,224,384]{2,1,0:T(8,128)(2,1)S(1)}, u32[]{:S(2)}, u32[]{:S(2)}) async-start(bf16[8,224,384]{2,1,0:T(8,128)(2,1)} %copy-done), calls=%async_computation.7 | async-start | bytes 2752512 | tf_op jit(solution)/shard_map/all_to_all | solution.py:427
  166.2 0.1 select_reduce_fusion
  166.3 0.5 fusion
  166.8 0.2 broadcast_in_dim.40.diagonal_ref
  167.0 19.9 %all-to-all-done.7.got_ref = bf16[8,224,384]{2,1,0:T(8,128)(2,1)S(1)} async-done(((bf16[8,224,384]{2,1,0:T(8,128)(2,1)}), bf16[8,224,384]{2,1,0:T(8,128)(2,1)S(1)}, u32[]{:S(2)}, u32[]{:S(2)}) %all-to-all-start.7) | async-done | bytes 1376288 | tf_op jit(solution)/shard_map/all_to_all | solution.py:427
  186.9 1.3 copy-done.2
  188.1 3.6 %final_kernel.1 = (bf16[320,384]{1,0:T(8,128)(2,1)}, bf16[320,384]{1,0:T(8,128)(2,1)}, f32[768,384]{1,0:T(8,128)}) custom-call(s32[2]{0:T(128)S(1)} %pad_add_fusion.place_ref, s32[8,8]{1,0:T(8,128)S(1)} %copy-done.11, bf16[8,224,384]{2,1,0:T(8,128)(2,1)S(1)} %all-to-all-done.7.got_ref, bf16[1024,768]{1,0:T(8,128)(2,1)S(1)} %bitcast.24, ...), custom_call_target="tpu_custom_call" | custom-call | flops 1048576 | bytes 65536 | tf_op jit(solution)/shard_map/final_kernel/pallas_call | solution.py:320
  (22 shorter events, 0.1 us)
Async XLA Ops:
  0.6 19.8 %copy-start.11 = (s32[8,8]{1,0:T(8,128)S(1)}, s32[8,8]{1,0:T(8,128)}, u32[]{:S(2)}) copy-start(s32[8,8]{1,0:T(8,128)} %lengths_ref.7) | copy-start | bytes 772
  0.7 0.9 copy-start.8
  1.7 0.9 copy-start.9
  2.6 0.7 copy-start.10
  20.4 7.0 %copy-start.1 = (f32[768,384]{1,0:T(8,128)S(1)}, f32[768,384]{1,0:T(8,128)}, u32[]{:S(2)}) copy-start(f32[768,384]{1,0:T(8,128)} %matrix_ref.1) | copy-start | bytes 3538948
  21.6 1.3 collective-permute-start
  23.9 16.9 %all-to-all-start.1 = ((bf16[8,64,768]{2,1,0:T(8,128)(2,1)}), bf16[8,64,768]{2,1,0:T(8,128)(2,1)S(1)}, u32[]{:S(2)}, u32[]{:S(2)}) async-start(bf16[8,64,768]{2,1,0:T(8,128)(2,1)} %broadcast_in_dim.28), calls=%async_computation.1 | async-start | bytes 1572864 | tf_op jit(solution)/shard_map/all_to_all | solution.py:358
  28.4 13.2 %copy-start.6 = (bf16[768,384]{1,0:T(8,128)(2,1)}, bf16[768,384]{1,0:T(8,128)(2,1)S(1)}, u32[]{:S(2)}) copy-start(bf16[768,384]{1,0:T(8,128)(2,1)S(1)} %get-tuple-element.28.high_ref) | copy-start | bytes 1769476
  28.4 12.3 %collective-permute-start.1 = (bf16[768,384]{1,0:T(8,128)(2,1)S(1)}, bf16[768,384]{1,0:T(8,128)(2,1)S(1)}, u32[]{:S(2)}, u32[]{:S(2)}) collective-permute-start(bf16[768,384]{1,0:T(8,128)(2,1)S(1)} %get-tuple-element.28.high_ref), channel_id=1, source_target_pairs={{0,1},{1,0},{2,3},{3,2},{4,5},{5,4},{6,7},{7,6},{8,9},{9,8},{10,11... | collective-permute-start | bytes 1769480 | tf_op jit(solution)/shard_map/ppermute | solution.py:61
  79.6 23.7 %all-to-all-start.4 = ((bf16[8,128,768]{2,1,0:T(8,128)(2,1)}), bf16[8,128,768]{2,1,0:T(8,128)(2,1)}, u32[]{:S(2)}, u32[]{:S(2)}) async-start(bf16[8,128,768]{2,1,0:T(8,128)(2,1)} %broadcast_in_dim.30), calls=%async_computation.4 | async-start | bytes 3145728 | tf_op jit(solution)/shard_map/all_to_all | solution.py:384
  86.4 2.3 %collective-permute-start.2 = (bf16[8,64,768]{2,1,0:T(8,128)(2,1)S(1)}, bf16[8,64,768]{2,1,0:T(8,128)(2,1)S(1)}, u32[]{:S(2)}, u32[]{:S(2)}) collective-permute-start(bf16[8,64,768]{2,1,0:T(8,128)(2,1)S(1)} %get-tuple-element.25.near_ref), channel_id=1, source_target_pairs={{0,1},{1,0},{2,3},{3,2},{4,5},{5,4},{6,7},{7,6},{8,9},{9,8},{10,11... | collective-permute-start | bytes 2359304 | tf_op jit(solution)/shard_map/ppermute | solution.py:61
  103.4 4.0 %copy-start.5 = (bf16[768,384]{1,0:T(8,128)(2,1)S(1)}, bf16[768,384]{1,0:T(8,128)(2,1)}, u32[]{:S(2)}) copy-start(bf16[768,384]{1,0:T(8,128)(2,1)} %get-tuple-element.27.low_ref) | copy-start | bytes 1769476
  103.4 4.0 %copy-start.7 = (bf16[768,384]{1,0:T(8,128)(2,1)S(1)}, bf16[768,384]{1,0:T(8,128)(2,1)}, u32[]{:S(2)}) copy-start(bf16[768,384]{1,0:T(8,128)(2,1)} %copy-done.6) | copy-start | bytes 1769476
  105.0 2.4 %collective-permute-start.3 = (bf16[64,6144]{1,0:T(8,128)(2,1)S(1)}, bf16[64,6144]{1,0:T(8,128)(2,1)S(1)}, u32[]{:S(2)}, u32[]{:S(2)}) collective-permute-start(bf16[64,6144]{1,0:T(8,128)(2,1)S(1)} %bitcast.27), channel_id=1, source_target_pairs={{0,1},{1,0},{2,3},{3,2},{4,5},{5,4},{6,7},{7,6},{8,9},{9,8},{10,11... | collective-permute-start | bytes 2359304 | tf_op jit(solution)/shard_map/ppermute | solution.py:61
  105.0 9.4 %collective-permute-start.4 = (bf16[64,6144]{1,0:T(8,128)(2,1)S(1)}, bf16[64,6144]{1,0:T(8,128)(2,1)S(1)}, u32[]{:S(2)}, u32[]{:S(2)}) collective-permute-start(bf16[64,6144]{1,0:T(8,128)(2,1)S(1)} %bitcast.25), channel_id=1, source_target_pairs={{0,1},{1,0},{2,3},{3,2},{4,5},{5,4},{6,7},{7,6},{8,9},{9,8},{10,11... | collective-permute-start | bytes 2359304 | tf_op jit(solution)/shard_map/ppermute | solution.py:61
  109.2 0.9 copy-start.4
  110.1 17.6 %all-to-all-start.5 = ((bf16[8,128,384]{2,1,0:T(8,128)(2,1)}), bf16[8,128,384]{2,1,0:T(8,128)(2,1)}, u32[]{:S(2)}, u32[]{:S(2)}) async-start(bf16[8,128,384]{2,1,0:T(8,128)(2,1)} %copy-done.4), calls=%async_computation.5 | async-start | bytes 1572864 | tf_op jit(solution)/shard_map/all_to_all | solution.py:403
  123.7 1.2 copy-start.3
  124.9 1.1 copy-start.12
  127.7 3.6 %collective-permute-start.5 = (bf16[8,256,384]{2,1,0:T(8,128)(2,1)}, bf16[8,256,384]{2,1,0:T(8,128)(2,1)S(1)}, u32[]{:S(2)}, u32[]{:S(2)}) collective-permute-start(bf16[8,256,384]{2,1,0:T(8,128)(2,1)} %copy-done.12), channel_id=1, source_target_pairs={{0,1},{1,0},{2,3},{3,2},{4,5},{5,4},{6,7},{7,6},{8,9},{9,8},{10,11... | collective-permute-start | bytes 4718600 | tf_op jit(solution)/shard_map/ppermute | solution.py:61
  134.3 25.8 %all-to-all-start.6 = ((bf16[8,256,384]{2,1,0:T(8,128)(2,1)}), bf16[8,256,384]{2,1,0:T(8,128)(2,1)S(1)}, u32[]{:S(2)}, u32[]{:S(2)}) async-start(bf16[8,256,384]{2,1,0:T(8,128)(2,1)} %add_convert_fusion), calls=%async_computation.6 | async-start | bytes 3145728 | tf_op jit(solution)/shard_map/all_to_all | solution.py:415
  161.3 1.1 copy-start
  162.4 24.5 %all-to-all-start.7 = ((bf16[8,224,384]{2,1,0:T(8,128)(2,1)}), bf16[8,224,384]{2,1,0:T(8,128)(2,1)S(1)}, u32[]{:S(2)}, u32[]{:S(2)}) async-start(bf16[8,224,384]{2,1,0:T(8,128)(2,1)} %copy-done), calls=%async_computation.7 | async-start | bytes 2752512 | tf_op jit(solution)/shard_map/all_to_all | solution.py:427
  186.9 1.3 copy-start.2

commit v5 on v4

--- a/solution.py
+++ b/solution.py
@@ -298,17 +298,16 @@
     live, starts = rank_spans(lengths_ref)
     start, own_live = entry_of(starts, place_ref[0]), entry_of(live, place_ref[0])
     row_total, width = out_ref.shape
-    row = lax.broadcasted_iota(jnp.int32, (row_total, SLOTS), 0)
-    slot = lax.broadcasted_iota(jnp.int32, (row_total, SLOTS), 1)
-    out_total = jnp.zeros((row_total, width), F32)
-    grad_total = jnp.zeros((row_total, width), F32)
+    row = lax.broadcasted_iota(jnp.int32, (row_total, N_DP * SLOTS), 0)
+    place = lax.broadcasted_iota(jnp.int32, (1, N_DP * SLOTS), 1)
+    wanted = jnp.zeros_like(place)
     for group in range(N_DP):
-        wanted = slot * N_DP + first_row(group, start)
-        pick = one_hot((row == wanted) & (row < own_live))
-        out_total = out_total + dot(pick, got_ref[group, pl.ds(0, SLOTS), :])
-        grad_total = grad_total + dot(pick, got_ref[group, pl.ds(SLOTS, SLOTS), :])
-    out_ref[...] = out_total.astype(BF16)
-    grad_ref[...] = grad_total.astype(BF16)
+        here = (place - group * SLOTS) * N_DP + first_row(group, start)
+        wanted = jnp.where(place >= group * SLOTS, here, wanted)
+    pick = one_hot((row == wanted) & (row < own_live))
+    for target, offset in ((out_ref, 0), (grad_ref, SLOTS)):
+        rows = got_ref[:, pl.ds(offset, SLOTS), :].reshape(N_DP * SLOTS, width)
+        target[...] = dot(pick, rows).astype(BF16)
     mixed = got_ref[:, pl.ds(2 * SLOTS, GROUP), :].reshape(ROWS, width)
     product = dot(rows_ref[...], mixed, CONTRACT_FIRST)
     step_ref[...] = product - diagonal_ref[...] * matrix_ref[...]

time: 193 us -> 192 us (level)
  no operation moved by 1% of the time
where the time goes in v5:
time: 192 us; the launch traced here: 191 us
  waiting for transfers between devices  69.4 us (36%)
  blocking collectives  52.1 us (27%)
  starting transfers between devices  25 us (13%)
  Pallas kernels  24.1 us (13%)
  local copies, waits for them, and re-layouts  12.3 us (6%)
  other arithmetic  6.54 us (3%)
    all_to_all x2, waiting for transfers between devices, local(): got = lax.all_to_all(sent, DP, 0, 0, tiled=True)  32 us
    all_to_all x1, blocking collectives, local(): got = lax.all_to_all(sent, CHIPS, 0, 0, tiled=True)  27.4 us
    all_to_all x1, waiting for transfers between devices, local(): got = lax.all_to_all(summed, CHIPS, 0, 0, tiled=True)  18.3 us
    all_to_all x1, blocking collectives, local(): got = lax.all_to_all(sent, DP, 0, 0, tiled=True)  15.6 us
    pallas_call x1, Pallas kernels, feed_forward(): pl.pallas_call(feed_kernel, in_specs=[pl.BlockSpec(memory_space=pltpu.SME...  9.19 us
    all_to_all x1, blocking collectives, local(): white_part = lax.all_to_all(white_chunk, DP, 0, 0, tiled=True)  9.04 us
    ppermute x6, waiting for transfers between devices, swap_core(): return lax.ppermute(value, CORE, [(0, 1), (1, 0)])  8.9 us
    all_to_all x1, waiting for transfers between devices, local(): got = lax.all_to_all(sent, CHIPS, 0, 0, tiled=True)  8.47 us
  transfers between devices with their start and end apart: 11, of which 9 were waited for; matrix products, arithmetic and copies ran while one was open for 2% of the time, Pallas kernels for 9%

profile of v5, /device:TPU:16, one launch (start us, length us, event | category | flops | bytes accessed | tf_op | source)
XLA Modules:
  0.0 191.1 jit_solution(11089478376910856333)
XLA Ops:
  0.6 0.0 copy-start.11
  0.6 0.1 pad_add_fusion.place_ref
  0.7 0.9 copy-done.8
  1.7 0.9 copy-done.9
  2.6 0.7 copy-done.10
  3.3 1.4 pack_kernel.1
  4.7 15.6 %all_to_all.40.got_ref = bf16[8,48,768]{2,1,0:T(8,128)(2,1)S(1)} all-to-all(bf16[8,48,768]{2,1,0:T(8,128)(2,1)S(1)} %pack_kernel.1), channel_id=1, replica_groups=mesh['x'=4,'yl'=2,'yh'=2,'z'=4,'core'=2] {'x','yl'}, dimensions={0} | all-to-all | bytes 1179648 | tf_op jit(solution)/shard_map/all_to_all | solution.py:344
  20.4 0.0 copy-done.11
  20.4 1.2 group_kernel.1
  21.6 0.1 collective-permute-start
  21.7 1.2 collective-permute-done
  22.9 0.9 broadcast_in_dim.28
  23.9 3.5 %all-to-all-start.1 = ((bf16[8,64,768]{2,1,0:T(8,128)(2,1)}), bf16[8,64,768]{2,1,0:T(8,128)(2,1)S(1)}, u32[]{:S(2)}, u32[]{:S(2)}) async-start(bf16[8,64,768]{2,1,0:T(8,128)(2,1)} %broadcast_in_dim.28), calls=%async_computation.1 | async-start | bytes 1572864 | tf_op jit(solution)/shard_map/all_to_all | solution.py:357
  27.4 1.0 fusion.1
  28.4 0.2 collective-permute-start.1
  28.6 12.1 %all-to-all-done.1 = bf16[8,64,768]{2,1,0:T(8,128)(2,1)S(1)} async-done(((bf16[8,64,768]{2,1,0:T(8,128)(2,1)}), bf16[8,64,768]{2,1,0:T(8,128)(2,1)S(1)}, u32[]{:S(2)}, u32[]{:S(2)}) %all-to-all-start.1) | async-done | bytes 786464 | tf_op jit(solution)/shard_map/all_to_all | solution.py:357
  40.7 0.1 copy.15
  40.8 0.0 collective-permute-done.1
  40.8 0.8 convolution_convert_fusion
  41.6 0.1 broadcast_in_dim.29
  41.7 0.1 pad_maximum_fusion
  41.8 27.4 %all_to_all.41 = bf16[8,128,768]{2,1,0:T(8,128)(2,1)S(1)} all-to-all(bf16[8,128,768]{2,1,0:T(8,128)(2,1)S(1)} %pad_maximum_fusion), channel_id=1, replica_groups=mesh['x'=4,'yl'=2,'yh'=2,'z'=4,'core'=2] {'yh','z'}, dimensions={0} | all-to-all | bytes 3145728 | tf_op jit(solution)/shard_map/all_to_all | solution.py:372
  69.2 0.1 fusion.7
  69.3 9.0 %all_to_all.42 = bf16[8,8,768]{2,1,0:T(8,128)(2,1)S(1)} all-to-all(bf16[8,8,768]{2,1,0:T(8,128)(2,1)S(1)} %bitcast.30), channel_id=1, replica_groups=mesh['x'=4,'yl'=2,'yh'=2,'z'=4,'core'=2] {'x','yl'}, dimensions={0} | all-to-all | bytes 196608 | tf_op jit(solution)/shard_map/all_to_all | solution.py:377
  78.4 1.2 broadcast_in_dim.30
  79.6 6.8 %all-to-all-start.4 = ((bf16[8,128,768]{2,1,0:T(8,128)(2,1)}), bf16[8,128,768]{2,1,0:T(8,128)(2,1)}, u32[]{:S(2)}, u32[]{:S(2)}) async-start(bf16[8,128,768]{2,1,0:T(8,128)(2,1)} %broadcast_in_dim.30), calls=%async_computation.4 | async-start | bytes 3145728 | tf_op jit(solution)/shard_map/all_to_all | solution.py:383
  86.4 0.0 collective-permute-start.2
  86.4 2.3 %collective-permute-done.2.far_ref = bf16[8,64,768]{2,1,0:T(8,128)(2,1)S(1)} collective-permute-done((bf16[8,64,768]{2,1,0:T(8,128)(2,1)S(1)}, bf16[8,64,768]{2,1,0:T(8,128)(2,1)S(1)}, u32[]{:S(2)}, u32[]{:S(2)}) %collective-permute-start.2) | collective-permute-done | bytes 786464 | tf_op jit(solution)/shard_map/ppermute | solution.py:61
  88.7 6.2 %back_terms.1.back_ref = f32[128,768]{1,0:T(8,128)S(1)} custom-call(s32[1]{0:T(128)} %bitcast.1.core_ref, bf16[8,64,768]{2,1,0:T(8,128)(2,1)S(1)} %get-tuple-element.25.near_ref, bf16[8,64,768]{2,1,0:T(8,128)(2,1)S(1)} %collective-permute-done.2.far_ref, bf16[768,6144]{1,0:T(8,128)(2,1)} %out_ref.3), custom_call_target="tpu_custom_call" | custom-call | flops 1048576 | bytes 65536 | tf_op jit(solution)/shard_map/back_terms/pallas_call | solution.py:199
  94.9 8.5 %all-to-all-done.4 = bf16[8,128,768]{2,1,0:T(8,128)(2,1)} async-done(((bf16[8,128,768]{2,1,0:T(8,128)(2,1)}), bf16[8,128,768]{2,1,0:T(8,128)(2,1)}, u32[]{:S(2)}, u32[]{:S(2)}) %all-to-all-start.4) | async-done | bytes 1572896 | tf_op jit(solution)/shard_map/all_to_all | solution.py:383
  103.4 1.6 fusion.6
  105.0 0.1 collective-permute-start.3
  105.0 0.5 collective-permute-start.4
  105.5 1.8 collective-permute-done.3.far_ref
  107.3 1.9 mixed_terms.1
  109.2 0.0 copy-start.4
  109.2 0.9 copy-done.4
  110.1 4.4 %all-to-all-start.5 = ((bf16[8,128,384]{2,1,0:T(8,128)(2,1)}), bf16[8,128,384]{2,1,0:T(8,128)(2,1)}, u32[]{:S(2)}, u32[]{:S(2)}) async-start(bf16[8,128,384]{2,1,0:T(8,128)(2,1)} %copy-done.4), calls=%async_computation.5 | async-start | bytes 1572864 | tf_op jit(solution)/shard_map/all_to_all | solution.py:402
  114.5 0.0 collective-permute-done.4.far_ref
  114.5 9.2 %feed_forward.1 = (bf16[8,256,384]{2,1,0:T(8,128)(2,1)S(1)}, bf16[8,256,384]{2,1,0:T(8,128)(2,1)S(1)}) custom-call(s32[1]{0:T(128)} %bitcast.1.core_ref, bf16[64,6144]{1,0:T(8,128)(2,1)S(1)} %bitcast.26, bf16[64,6144]{1,0:T(8,128)(2,1)S(1)} %collective-permute-done.4.far_ref, f32[128,768]{1,0:T(8,128)S(1)} %back_terms.1.back_ref, bf16[6144,768]{1,0:T(8,128)(2,1)} %in_ref.1, ...), custom_call_target="tpu_custom_call" | custom-call | flops 1048576 | bytes 65536 | tf_op jit(solution)/shard_map/feed_forward/pallas_call | solution.py:152
  123.7 1.2 copy-done.3
  124.9 1.1 copy-done.12
  126.0 1.7 all-to-all-done.5
  127.7 0.0 collective-permute-start.5
  127.7 3.6 %collective-permute-done.5 = bf16[8,256,384]{2,1,0:T(8,128)(2,1)S(1)} collective-permute-done((bf16[8,256,384]{2,1,0:T(8,128)(2,1)}, bf16[8,256,384]{2,1,0:T(8,128)(2,1)S(1)}, u32[]{:S(2)}, u32[]{:S(2)}) %collective-permute-start.5) | collective-permute-done | bytes 1572896 | tf_op jit(solution)/shard_map/ppermute | solution.py:61
  131.3 2.9 %add_convert_fusion = bf16[8,256,384]{2,1,0:T(8,128)(2,1)} fusion(bf16[8,256,384]{2,1,0:T(8,128)(2,1)S(1)} %collective-permute-done.5, bf16[8,256,384]{2,1,0:T(8,128)(2,1)} %copy-done.3), kind=kLoop, calls=%fused_computation.2 | loop fusion | flops 3145728 | bytes 4718592 | tf_op jit(solution)/shard_map/convert_element_type | solution.py:413
  134.3 5.7 %all-to-all-start.6 = ((bf16[8,256,384]{2,1,0:T(8,128)(2,1)}), bf16[8,256,384]{2,1,0:T(8,128)(2,1)S(1)}, u32[]{:S(2)}, u32[]{:S(2)}) async-start(bf16[8,256,384]{2,1,0:T(8,128)(2,1)} %add_convert_fusion), calls=%async_computation.6 | async-start | bytes 3145728 | tf_op jit(solution)/shard_map/all_to_all | solution.py:414
  139.9 0.1 reshape.122
  140.0 0.1 reshape.120
  140.1 0.1 reduce-window.7
  140.2 0.1 reduce.2
  140.3 0.1 select_reduce_fusion.1
  140.4 1.3 convert_reduce_fusion
  141.7 0.1 multiply_convert_fusion.mixed_ref
  141.8 18.3 %all-to-all-done.6.got_ref = bf16[8,256,384]{2,1,0:T(8,128)(2,1)S(1)} async-done(((bf16[8,256,384]{2,1,0:T(8,128)(2,1)}), bf16[8,256,384]{2,1,0:T(8,128)(2,1)S(1)}, u32[]{:S(2)}, u32[]{:S(2)}) %all-to-all-start.6) | async-done | bytes 1572896 | tf_op jit(solution)/shard_map/all_to_all | solution.py:414
  160.1 1.2 spread_kernel.1
  161.3 1.1 copy-done
  162.4 3.8 %all-to-all-start.7 = ((bf16[8,224,384]{2,1,0:T(8,128)(2,1)}), bf16[8,224,384]{2,1,0:T(8,128)(2,1)S(1)}, u32[]{:S(2)}, u32[]{:S(2)}) async-start(bf16[8,224,384]{2,1,0:T(8,128)(2,1)} %copy-done), calls=%async_computation.7 | async-start | bytes 2752512 | tf_op jit(solution)/shard_map/all_to_all | solution.py:426
  166.2 0.1 select_reduce_fusion
  166.3 0.5 fusion
  166.8 0.2 broadcast_in_dim.40.diagonal_ref
  167.0 19.9 %all-to-all-done.7.got_ref = bf16[8,224,384]{2,1,0:T(8,128)(2,1)S(1)} async-done(((bf16[8,224,384]{2,1,0:T(8,128)(2,1)}), bf16[8,224,384]{2,1,0:T(8,128)(2,1)S(1)}, u32[]{:S(2)}, u32[]{:S(2)}) %all-to-all-start.7) | async-done | bytes 1376288 | tf_op jit(solution)/shard_map/all_to_all | solution.py:426
  186.9 1.3 copy-done.2
  188.1 2.9 %final_kernel.1 = (bf16[320,384]{1,0:T(8,128)(2,1)}, bf16[320,384]{1,0:T(8,128)(2,1)}, f32[768,384]{1,0:T(8,128)}) custom-call(s32[2]{0:T(128)S(1)} %pad_add_fusion.place_ref, s32[8,8]{1,0:T(8,128)S(1)} %copy-done.11, bf16[8,224,384]{2,1,0:T(8,128)(2,1)S(1)} %all-to-all-done.7.got_ref, bf16[1024,768]{1,0:T(8,128)(2,1)S(1)} %bitcast.24, ...), custom_call_target="tpu_custom_call" | custom-call | flops 1048576 | bytes 65536 | tf_op jit(solution)/shard_map/final_kernel/pallas_call | solution.py:319
  (22 shorter events, 0.1 us)
Async XLA Ops:
  0.6 19.8 %copy-start.11 = (s32[8,8]{1,0:T(8,128)S(1)}, s32[8,8]{1,0:T(8,128)}, u32[]{:S(2)}) copy-start(s32[8,8]{1,0:T(8,128)} %lengths_ref.7) | copy-start | bytes 772
  0.7 0.9 copy-start.8
  1.7 0.9 copy-start.9
  2.6 0.7 copy-start.10
  20.4 7.0 %copy-start.1 = (f32[768,384]{1,0:T(8,128)S(1)}, f32[768,384]{1,0:T(8,128)}, u32[]{:S(2)}) copy-start(f32[768,384]{1,0:T(8,128)} %matrix_ref.1) | copy-start | bytes 3538948
  21.6 1.3 collective-permute-start
  23.9 16.9 %all-to-all-start.1 = ((bf16[8,64,768]{2,1,0:T(8,128)(2,1)}), bf16[8,64,768]{2,1,0:T(8,128)(2,1)S(1)}, u32[]{:S(2)}, u32[]{:S(2)}) async-start(bf16[8,64,768]{2,1,0:T(8,128)(2,1)} %broadcast_in_dim.28), calls=%async_computation.1 | async-start | bytes 1572864 | tf_op jit(solution)/shard_map/all_to_all | solution.py:357
  28.4 13.2 %copy-start.6 = (bf16[768,384]{1,0:T(8,128)(2,1)}, bf16[768,384]{1,0:T(8,128)(2,1)S(1)}, u32[]{:S(2)}) copy-start(bf16[768,384]{1,0:T(8,128)(2,1)S(1)} %get-tuple-element.28.high_ref) | copy-start | bytes 1769476
  28.4 12.3 %collective-permute-start.1 = (bf16[768,384]{1,0:T(8,128)(2,1)S(1)}, bf16[768,384]{1,0:T(8,128)(2,1)S(1)}, u32[]{:S(2)}, u32[]{:S(2)}) collective-permute-start(bf16[768,384]{1,0:T(8,128)(2,1)S(1)} %get-tuple-element.28.high_ref), channel_id=1, source_target_pairs={{0,1},{1,0},{2,3},{3,2},{4,5},{5,4},{6,7},{7,6},{8,9},{9,8},{10,11... | collective-permute-start | bytes 1769480 | tf_op jit(solution)/shard_map/ppermute | solution.py:61
  79.6 23.7 %all-to-all-start.4 = ((bf16[8,128,768]{2,1,0:T(8,128)(2,1)}), bf16[8,128,768]{2,1,0:T(8,128)(2,1)}, u32[]{:S(2)}, u32[]{:S(2)}) async-start(bf16[8,128,768]{2,1,0:T(8,128)(2,1)} %broadcast_in_dim.30), calls=%async_computation.4 | async-start | bytes 3145728 | tf_op jit(solution)/shard_map/all_to_all | solution.py:383
  86.4 2.3 %collective-permute-start.2 = (bf16[8,64,768]{2,1,0:T(8,128)(2,1)S(1)}, bf16[8,64,768]{2,1,0:T(8,128)(2,1)S(1)}, u32[]{:S(2)}, u32[]{:S(2)}) collective-permute-start(bf16[8,64,768]{2,1,0:T(8,128)(2,1)S(1)} %get-tuple-element.25.near_ref), channel_id=1, source_target_pairs={{0,1},{1,0},{2,3},{3,2},{4,5},{5,4},{6,7},{7,6},{8,9},{9,8},{10,11... | collective-permute-start | bytes 2359304 | tf_op jit(solution)/shard_map/ppermute | solution.py:61
  103.4 4.0 %copy-start.5 = (bf16[768,384]{1,0:T(8,128)(2,1)S(1)}, bf16[768,384]{1,0:T(8,128)(2,1)}, u32[]{:S(2)}) copy-start(bf16[768,384]{1,0:T(8,128)(2,1)} %get-tuple-element.27.low_ref) | copy-start | bytes 1769476
  103.4 4.0 %copy-start.7 = (bf16[768,384]{1,0:T(8,128)(2,1)S(1)}, bf16[768,384]{1,0:T(8,128)(2,1)}, u32[]{:S(2)}) copy-start(bf16[768,384]{1,0:T(8,128)(2,1)} %copy-done.6) | copy-start | bytes 1769476
  105.0 2.4 %collective-permute-start.3 = (bf16[64,6144]{1,0:T(8,128)(2,1)S(1)}, bf16[64,6144]{1,0:T(8,128)(2,1)S(1)}, u32[]{:S(2)}, u32[]{:S(2)}) collective-permute-start(bf16[64,6144]{1,0:T(8,128)(2,1)S(1)} %bitcast.27), channel_id=1, source_target_pairs={{0,1},{1,0},{2,3},{3,2},{4,5},{5,4},{6,7},{7,6},{8,9},{9,8},{10,11... | collective-permute-start | bytes 2359304 | tf_op jit(solution)/shard_map/ppermute | solution.py:61
  105.0 9.4 %collective-permute-start.4 = (bf16[64,6144]{1,0:T(8,128)(2,1)S(1)}, bf16[64,6144]{1,0:T(8,128)(2,1)S(1)}, u32[]{:S(2)}, u32[]{:S(2)}) collective-permute-start(bf16[64,6144]{1,0:T(8,128)(2,1)S(1)} %bitcast.25), channel_id=1, source_target_pairs={{0,1},{1,0},{2,3},{3,2},{4,5},{5,4},{6,7},{7,6},{8,9},{9,8},{10,11... | collective-permute-start | bytes 2359304 | tf_op jit(solution)/shard_map/ppermute | solution.py:61
  109.2 0.9 copy-start.4
  110.1 17.6 %all-to-all-start.5 = ((bf16[8,128,384]{2,1,0:T(8,128)(2,1)}), bf16[8,128,384]{2,1,0:T(8,128)(2,1)}, u32[]{:S(2)}, u32[]{:S(2)}) async-start(bf16[8,128,384]{2,1,0:T(8,128)(2,1)} %copy-done.4), calls=%async_computation.5 | async-start | bytes 1572864 | tf_op jit(solution)/shard_map/all_to_all | solution.py:402
  123.7 1.2 copy-start.3
  124.9 1.1 copy-start.12
  127.7 3.6 %collective-permute-start.5 = (bf16[8,256,384]{2,1,0:T(8,128)(2,1)}, bf16[8,256,384]{2,1,0:T(8,128)(2,1)S(1)}, u32[]{:S(2)}, u32[]{:S(2)}) collective-permute-start(bf16[8,256,384]{2,1,0:T(8,128)(2,1)} %copy-done.12), channel_id=1, source_target_pairs={{0,1},{1,0},{2,3},{3,2},{4,5},{5,4},{6,7},{7,6},{8,9},{9,8},{10,11... | collective-permute-start | bytes 4718600 | tf_op jit(solution)/shard_map/ppermute | solution.py:61
  134.3 25.8 %all-to-all-start.6 = ((bf16[8,256,384]{2,1,0:T(8,128)(2,1)}), bf16[8,256,384]{2,1,0:T(8,128)(2,1)S(1)}, u32[]{:S(2)}, u32[]{:S(2)}) async-start(bf16[8,256,384]{2,1,0:T(8,128)(2,1)} %add_convert_fusion), calls=%async_computation.6 | async-start | bytes 3145728 | tf_op jit(solution)/shard_map/all_to_all | solution.py:414
  161.3 1.1 copy-start
  162.4 24.5 %all-to-all-start.7 = ((bf16[8,224,384]{2,1,0:T(8,128)(2,1)}), bf16[8,224,384]{2,1,0:T(8,128)(2,1)S(1)}, u32[]{:S(2)}, u32[]{:S(2)}) async-start(bf16[8,224,384]{2,1,0:T(8,128)(2,1)} %copy-done), calls=%async_computation.7 | async-start | bytes 2752512 | tf_op jit(solution)/shard_map/all_to_all | solution.py:426
  186.9 1.3 copy-start.2
